TPU v7x, 256 devices: a whole 4x4x8 slice. The times are simulated.
256 devices in a mesh: grp: 16 (over y, x_hi, core), sh: 16 (over z, x_lo).
Axes of the slice: x: 4 (x_hi: 2, x_lo: 2; x = x_hi * 2 + x_lo), y: 4, z: 8, core: 2. Of those that a mesh axis runs over, the one named last changes fastest.
Arguments:
- factors: bfloat16 [48, 128, 14336], P('grp', None, 'sh'), may hold values from -0.5 to 0.5
- screen: int32 [48, 1, 112], P('grp', None, 'sh'), may hold values 0 or 1
- occ_energy: float32 [48], replicated, may hold values from -1.5 to -0.3
- virt_energy: float32 [128], replicated, may hold values from 0.5 to 3
Outputs:
- gamma: bfloat16 [48, 128, 14336], P('grp', 'sh')
Inputs may be any that keep to these rules, and one draw needn't show every extreme that they name: `screen`: 1 keeps a block of 128 virtual by 128 auxiliary functions of one occupied orbital, 0 screens it out.
All inputs are finite; a program needn't handle non-finite values.
Results may differ from a plain program's by a relative error of at most 0.0049.
Values may be sent and summed in bfloat16 or wider, within the bound.
No kernel may reach another device: no remote copies, remote signals or barrier semaphores. Data moves between devices by JAX's collectives and lax.ppermute only.
A program may use at most 64 MiB of HBM per device.

v0:
```python
import functools

import jax
import jax.numpy as jnp
from jax import lax
from jax.experimental import pallas as pl
from jax.experimental.pallas import tpu as pltpu
from jax.sharding import Mesh, PartitionSpec as P

BLK = 128
NY, NXH, NC, NZ, NXL = 4, 2, 2, 8, 2
GRP = ("y", "xh", "core")
SH = ("z", "xl")
X = ("xh", "xl")
BF = jnp.bfloat16
COLUMNS = (0, 1, 3, 2)
F32 = jnp.float32


def flip_x(value, bits):
    return lax.ppermute(value, X, [(i, i ^ bits) for i in range(NXH * NXL)])


def shift(value, axis, steps):
    count = lax.axis_size(axis)
    return lax.ppermute(value, axis, [(i, (i + steps) % count) for i in range(count)])


def flip_core(value):
    return lax.ppermute(value, "core", [(0, 1), (1, 0)])


def dot_t(a, b):
    return lax.dot_general(a, b, (((1,), (1,)), ((), ())), preferred_element_type=F32)


def coulomb_kernel(own, xlf, bof, xh, *refs):
    near, far, (p0, p1, p2, p3, p5, p6, p7), refs = refs[0:3], refs[3:6], refs[6:13], refs[13:]
    send_up, send_down, keep_up, keep_down, stack_out, out, stack, left, sem = refs
    z, xl, c = lax.axis_index("z"), lax.axis_index("xl"), lax.axis_index("core")
    rows, half = own.shape

    def lay(target, row0, col0, piece):
        step = 64

        def body(n, carry):
            rows_at = pl.multiple_of(row0 + n * step, step)
            target[pl.ds(rows_at, step), col0:col0 + half] = piece[pl.ds(pl.multiple_of(n * step, step), step), :]
            return carry

        lax.fori_loop(0, piece.shape[0] // step, body, 0)

    for k, pieces in enumerate((near, far)):
        at = 0
        for piece in pieces:
            lay(stack, at, k * half, piece)
            at += piece.shape[0]
    copy = pltpu.make_async_copy(stack, stack_out, sem)
    copy.start()

    @pl.when(xl == c)
    def _():
        lay(left, 0, 0, own)
        lay(left, 0, half, far[0])
        lay(left, rows, 0, xh)
        lay(left, rows, half, bof)

    @pl.when(xl != c)
    def _():
        lay(left, 0, half, own)
        lay(left, 0, 0, xlf)
        lay(left, rows, half, xh)
        lay(left, rows, 0, bof)

    def block(n, carry):
        e, pair = n // 2, lax.rem(n, 2)
        got = dot_t(
            left[pl.ds(pl.multiple_of(e * rows, 128), rows), :],
            stack[pl.ds(pl.multiple_of(pair * 2 * rows, 128), 2 * rows), :],
        )
        for dd in range(2):
            out[lax.rem(e * NY + pair * 2 + dd + NZ - z, NZ)] = got[:, dd * rows:(dd + 1) * rows]
        return carry

    lax.fori_loop(0, NY, block, 0)
    low, high = slice(0, rows // 2), slice(rows // 2, rows)
    for k, ref in ((0, p0), (1, p1), (2, p2), (6, p6), (7, p7)):
        ref[...] = out[k]
    p3[...], p5[...] = out[3, low, :], out[5, high, :]
    send_up[...], send_down[...] = out[4, low, :].astype(BF), out[4, high, :].astype(BF)
    keep_up[...], keep_down[...] = out[3, high, :].astype(BF), out[5, low, :].astype(BF)
    copy.wait()


def combined_kernel(occ_ref, v_col, v_row, mine, up, down, out, scr):
    y, xh, c, z, xl = (lax.axis_index(n) for n in ("y", "xh", "core", "z", "xl"))
    virt = v_row.shape[1]
    count = mine.shape[0] // virt
    e, d = z // NY, lax.rem(z, NY)
    row_occ = ((y * NXH + lax.rem(xh + e, NXH)) * NC + c) * count
    back = jnp.where(d < 2, d, NY + 1 - d)
    col_occ = ((lax.rem(y + NY - back, NY) * NXH + xh) * NC + xl) * count
    for i in range(count):
        for j in range(count):
            tile = (pl.ds(i * virt, virt), pl.ds(j * virt, virt))
            total = mine[tile] + up[tile].astype(F32) + down[tile].astype(F32)
            row, col = v_col[...] - occ_ref[row_occ + i], v_row[...] - occ_ref[col_occ + j]
            amp = (total / (row + col)).astype(BF).astype(F32)
            comb = 2.0 * amp - amp.T
            for zp in range(NZ):
                for h in range(NXL):
                    at = (zp * NXL + h) * 8
                    scr[h, (zp * count + i) * 8:(zp * count + i + 1) * 8, j * virt:(j + 1) * virt] = comb[at:at + 8]
    for h in range(NXL):
        out[h] = scr[h].astype(BF)


def gamma_kernel(*refs, group):
    combs, stack, outs, (left, scr) = refs[0:9], refs[9], refs[10:-2], refs[-2:]
    half, rows = combs[0].shape[1:]
    z, xl = lax.axis_index("z"), lax.axis_index("xl")
    part = combs[7].shape[1]
    places = [(ref, step, 0) for ref, step in zip(combs[:7], (0, 1, -1, 2, -2, 3, -3))]
    for ref, step, row0 in places + [(combs[7], 4, 0), (combs[8], 4, part)]:
        source = lax.rem(z + NZ - step, NZ)

        @pl.when(source // NY == group)
        def _(ref=ref, source=source, row0=row0):
            cols = pl.ds(pl.multiple_of(lax.rem(source, NY) * rows, 128), rows)
            for fl in range(2):
                at = fl * half + row0
                left[at:at + ref.shape[1], cols] = ref[lax.rem(xl + fl, 2)]

    width = 2 * BLK
    piece = half // NZ

    def columns(n, carry):
        cols = pl.ds(pl.multiple_of(n * width, width), width)
        acc = jnp.dot(left[...], stack[:, cols], preferred_element_type=F32)
        for zp in range(NZ):
            at = lax.rem(zp + NZ - z, NZ)
            scr[0, at, :, cols] = acc[zp * piece:(zp + 1) * piece]
            scr[1, at, :, cols] = acc[half + zp * piece:half + (zp + 1) * piece]
        return carry

    lax.fori_loop(0, stack.shape[1] // width, columns, 0)
    n = NZ // 2
    for fl in range(2):
        for p in range(2):
            outs[2 * fl + p][...] = scr[fl, p * n:(p + 1) * n].astype(outs[2 * fl + p].dtype)


def assemble_kernel(*refs):
    out = refs[-1]
    z, core = lax.axis_index("z"), lax.axis_index("core")
    half = refs[0].shape[1] // 2
    for k in range(NZ):
        source = lax.rem(z + NZ - k, NZ)
        for part in range(2):
            start = pl.multiple_of(source * 2 * half + lax.rem(core + part, 2) * half, 128)
            out[:, pl.ds(start, half)] = refs[k][:, part * half:(part + 1) * half]


def on_device(factors, screen, occ_energy, virt_energy):
    occ_g, virt, aux = factors.shape
    rows = occ_g * virt
    hr = rows // 2
    wide_mask = jnp.repeat(jnp.repeat(screen, BLK, axis=1), BLK, axis=2)
    own = (factors * wide_mask.astype(BF)).reshape(rows, aux)

    with jax.named_scope("gather"):
        j0 = lax.ppermute(own, ("core", "xl"), [(0, 0), (1, 2), (2, 1), (3, 3)])
        bof = flip_x(own, 3)
        xlf = lax.ppermute(own, ("core", "xl"), [(0, 1), (3, 2)])
        j1, j3 = shift(j0, "y", 1), shift(j0, "y", -1)
        f0 = flip_core(j0)
        own_b, f0, xlf = lax.optimization_barrier((own, f0, xlf))
        xh = flip_x(own_b, 2)
        j1, j3, bof = lax.optimization_barrier((j1, j3, bof))
        j2a, j2b = shift(j1[:hr], "y", 1), shift(j3[hr:], "y", -1)
        j2a, j2b, xh = lax.optimization_barrier((j2a, j2b, xh))
        outer = jnp.concatenate([j1, j3])
        outer_far = flip_core(outer)
        inner = jnp.concatenate([j2a, j2b])
        inner_far = flip_core(inner)
        near, far = [j0, outer, inner], [f0, outer_far, inner_far]

    vmem = pl.BlockSpec(memory_space=pltpu.VMEM)
    smem = pl.BlockSpec(memory_space=pltpu.SMEM)
    params = pltpu.CompilerParams(vmem_limit_bytes=48 << 20)

    with jax.named_scope("coulomb"):
        whole, part = jax.ShapeDtypeStruct((rows, rows), F32), jax.ShapeDtypeStruct((hr, rows), F32)
        sent = jax.ShapeDtypeStruct((hr, rows), BF)
        mine, p1, p2, p3, p5, p6, p7, up, down, keep_up, keep_down, stack = pl.pallas_call(
            coulomb_kernel,
            out_shape=[whole, whole, whole, part, part, whole, whole, sent, sent, sent, sent]
            + [jax.ShapeDtypeStruct((NY * rows, 2 * aux), BF)],
            in_specs=[vmem] * 10,
            out_specs=[vmem] * 11 + [pl.BlockSpec(memory_space=pl.ANY)],
            scratch_shapes=[
                pltpu.VMEM((NZ, rows, rows), F32),
                pltpu.VMEM((NY * rows, 2 * aux), BF),
                pltpu.VMEM((2 * rows, 2 * aux), BF),
                pltpu.SemaphoreType.DMA,
            ],
            compiler_params=params,
        )(own, xlf, bof, xh, *near, *far)

    with jax.named_scope("ring"):
        up, down = shift(up, "z", 1), shift(down, "z", -1)
        up = jnp.concatenate([(up.astype(F32) + p3).astype(BF), keep_up])
        down = jnp.concatenate([keep_down, (down.astype(F32) + p5).astype(BF)])
        for from_up, from_down in ((p2, p6), (p1, p7), (None, None)):
            up, down = shift(up, "z", 1), shift(down, "z", -1)
            if from_up is not None:
                up = (up.astype(F32) + from_up).astype(BF)
                down = (down.astype(F32) + from_down).astype(BF)

    with jax.named_scope("combined"):
        comb = pl.pallas_call(
            combined_kernel,
            out_shape=jax.ShapeDtypeStruct((NXL, hr, rows), BF),
            in_specs=[smem] + [vmem] * 5,
            out_specs=vmem,
            scratch_shapes=[pltpu.VMEM((NXL, hr, rows), F32)],
            compiler_params=params,
        )(occ_energy, virt_energy[:, None], virt_energy[None, :], mine, up, down)
        up1, down1 = shift(comb, "z", 1), shift(comb, "z", -1)
        up2, down2 = shift(up1, "z", 1), shift(down1, "z", -1)
        up3, down3 = shift(up2, "z", 1), shift(down2, "z", -1)
        up4, down4 = shift(up3[:, :hr // 2], "z", 1), shift(down3[:, hr // 2:], "z", -1)
        combs = [comb, up1, down1, up2, down2, up3, down3, up4, down4]

    with jax.named_scope("gamma"):
        piece = hr // NZ

        def gamma_of(group, types):
            return pl.pallas_call(
                functools.partial(gamma_kernel, group=group),
                out_shape=[jax.ShapeDtypeStruct((NZ // 2, piece, 2 * aux), t) for t in types],
                in_specs=[vmem] * 10,
                out_specs=[vmem] * 4,
                scratch_shapes=[
                    pltpu.VMEM((2 * hr, NY * rows), BF),
                    pltpu.VMEM((2, NZ, piece, 2 * aux), F32),
                ],
                compiler_params=params,
            )(*combs, stack)

        to_xh0, to_xh1, to_both0, to_both1 = gamma_of(1, (BF, BF, BF, F32))
        via_both, via_xl = flip_x(to_xh0, 3), flip_x(to_xh1, 1)
        from_both0 = flip_x(to_both0, 3)
        mine0, mine1, to_xl0, to_xl1 = gamma_of(0, (F32, F32, F32, BF))
        via_both, via_xl, to_xl1 = lax.optimization_barrier((via_both, via_xl, to_xl1))
        from_xl1 = flip_x(to_xl1, 1)
        from_xl0 = flip_x((to_xl0 + via_both.astype(F32)).astype(BF), 1)
        from_both1 = flip_x((to_both1 + via_xl.astype(F32)).astype(BF), 3)
        first = (mine0 + from_xl0.astype(F32) + from_both0.astype(F32)).astype(BF)
        last = (mine1 + from_xl1.astype(F32) + from_both1.astype(F32)).astype(BF)
        total = [t[k] for t in (first, last) for k in range(NZ // 2)]

    with jax.named_scope("spread"):
        got = [total[0]] + [shift(total[k], "z", k) for k in range(1, NZ)]
        out = pl.pallas_call(
            assemble_kernel,
            out_shape=jax.ShapeDtypeStruct((piece, NZ * 2 * aux), BF),
            in_specs=[vmem] * NZ,
            out_specs=vmem,
            compiler_params=pltpu.CompilerParams(vmem_limit_bytes=16 << 20),
        )(*got)
    return out.reshape(occ_g, piece // occ_g, NZ * 2 * aux)


def solution(mesh):
    split = Mesh(mesh.devices.reshape(NY, NXH, NC, NZ, NXL), ("y", "xh", "core", "z", "xl"))
    placed = (P(GRP, None, SH), P(GRP, None, SH), P(), P())
    return jax.shard_map(on_device, mesh=split, in_specs=placed, out_specs=P(GRP, SH, None), check_vma=False)
```

profile of v0, /device:TPU:32, one launch (start us, length us, event | category | flops | bytes accessed | tf_op | source)
XLA Modules:
  0.0 187.4 jit_solution(7714522506883389988)
XLA Ops:
  2.7 4.3 %collective-permute-start.5 = (bf16[384,896]{1,0:T(8,128)(2,1)S(1)}, bf16[384,896]{1,0:T(8,128)(2,1)S(1)}, u32[]{:S(2)}, u32[]{:S(2)}) collective-permute-start(bf16[384,896]{1,0:T(8,128)(2,1)S(1)} %bitcast.29), channel_id=1, source_target_pairs={{0,33},{1,32},{32,1},{33,0},{2,35},{3,34},{34,3},{35,2},{4,37},{5,... | collective-permute-start | bytes 2064392 | tf_op jit(solution)/shard_map/gather/ppermute | solution.py:21
  10.2 10.6 %collective-permute-start.2 = (bf16[384,896]{1,0:T(8,128)(2,1)S(1)}, bf16[384,896]{1,0:T(8,128)(2,1)S(1)}, u32[]{:S(2)}, u32[]{:S(2)}) collective-permute-start(bf16[384,896]{1,0:T(8,128)(2,1)S(1)} %bitcast.30), channel_id=1, source_target_pairs={{0,1},{17,16},{2,3},{19,18},{4,5},{21,20},{6,7},{23,22},{8,9},{25,... | collective-permute-start | bytes 2064392 | tf_op jit(solution)/shard_map/gather/ppermute | solution.py:174
  22.5 6.8 %collective-permute-done.2.xlf = bf16[384,896]{1,0:T(8,128)(2,1)S(1)} collective-permute-done((bf16[384,896]{1,0:T(8,128)(2,1)S(1)}, bf16[384,896]{1,0:T(8,128)(2,1)S(1)}, u32[]{:S(2)}, u32[]{:S(2)}) %collective-permute-start.2) | collective-permute-done | bytes 688160 | tf_op jit(solution)/shard_map/gather/ppermute | solution.py:174
  35.7 8.4 %collective-permute-done.6 = bf16[192,896]{1,0:T(8,128)(2,1)S(1)} collective-permute-done((bf16[192,896]{1,0:T(8,128)(2,1)S(1)}, bf16[192,896]{1,0:T(8,128)(2,1)S(1)}, u32[]{:S(2)}, u32[]{:S(2)}) %collective-permute-start.6) | collective-permute-done | bytes 344096 | tf_op jit(solution)/shard_map/gather/ppermute | solution.py:26
  44.1 3.5 %collective-permute-done.8.xh = bf16[384,896]{1,0:T(8,128)(2,1)S(1)} collective-permute-done((bf16[384,896]{1,0:T(8,128)(2,1)S(1)}, bf16[384,896]{1,0:T(8,128)(2,1)S(1)}, u32[]{:S(2)}, u32[]{:S(2)}) %collective-permute-start.8) | collective-permute-done | bytes 688160 | tf_op jit(solution)/shard_map/gather/ppermute | solution.py:21
  52.0 9.0 %coulomb.1 = (f32[384,384]{1,0:T(8,128)S(1)}, f32[384,384]{1,0:T(8,128)S(1)}, f32[384,384]{1,0:T(8,128)S(1)}, f32[192,384]{1,0:T(8,128)S(1)}, f32[192,384]{1,0:T...) custom-call(bf16[384,896]{1,0:T(8,128)(2,1)S(1)} %bitcast.32, ...), custom_call_target="tpu_custom_call" | custom-call | tf_op jit(solution)/shard_map/coulomb/pallas_call | solution.py:195
  63.1 4.0 %collective-permute-done.15 = bf16[192,384]{1,0:T(8,128)(2,1)S(1)} collective-permute-done((bf16[192,384]{1,0:T(8,128)(2,1)S(1)}, bf16[192,384]{1,0:T(8,128)(2,1)S(1)}, u32[]{:S(2)}, u32[]{:S(2)}) %collective-permute-start.15) | collective-permute-done | bytes 147488 | tf_op jit(solution)/shard_map/ring/ppermute | solution.py:26
  67.3 3.4 %collective-permute-start.16 = (bf16[384,384]{1,0:T(8,128)(2,1)S(1)}, bf16[384,384]{1,0:T(8,128)(2,1)S(1)}, u32[]{:S(2)}, u32[]{:S(2)}) collective-permute-start(bf16[384,384]{1,0:T(8,128)(2,1)S(1)} %pad_maximum_fusion.1), channel_id=1, source_target_pairs={{0,14},{2,0},{4,2},{6,4},{8,6},{10,8},{12,10},{14,12},{1,15},{3,1}... | collective-permute-start | bytes 884744 | tf_op jit(solution)/shard_map/ring/ppermute | solution.py:26
  71.1 5.3 %collective-permute-done.16 = bf16[384,384]{1,0:T(8,128)(2,1)S(1)} collective-permute-done((bf16[384,384]{1,0:T(8,128)(2,1)S(1)}, bf16[384,384]{1,0:T(8,128)(2,1)S(1)}, u32[]{:S(2)}, u32[]{:S(2)}) %collective-permute-start.16) | collective-permute-done | bytes 294944 | tf_op jit(solution)/shard_map/ring/ppermute | solution.py:26
  76.5 3.8 %collective-permute-start.17 = (bf16[384,384]{1,0:T(8,128)(2,1)S(1)}, bf16[384,384]{1,0:T(8,128)(2,1)S(1)}, u32[]{:S(2)}, u32[]{:S(2)}) collective-permute-start(bf16[384,384]{1,0:T(8,128)(2,1)S(1)} %add_convert_fusion.5), channel_id=1, source_target_pairs={{0,14},{2,0},{4,2},{6,4},{8,6},{10,8},{12,10},{14,12},{1,15},{3,1}... | collective-permute-start | bytes 884744 | tf_op jit(solution)/shard_map/ring/ppermute | solution.py:26
  81.1 4.2 %collective-permute-done.17 = bf16[384,384]{1,0:T(8,128)(2,1)S(1)} collective-permute-done((bf16[384,384]{1,0:T(8,128)(2,1)S(1)}, bf16[384,384]{1,0:T(8,128)(2,1)S(1)}, u32[]{:S(2)}, u32[]{:S(2)}) %collective-permute-start.17) | collective-permute-done | bytes 294944 | tf_op jit(solution)/shard_map/ring/ppermute | solution.py:26
  85.4 3.5 %collective-permute-start.18 = (bf16[384,384]{1,0:T(8,128)(2,1)S(1)}, bf16[384,384]{1,0:T(8,128)(2,1)S(1)}, u32[]{:S(2)}, u32[]{:S(2)}) collective-permute-start(bf16[384,384]{1,0:T(8,128)(2,1)S(1)} %add_convert_fusion.4), channel_id=1, source_target_pairs={{0,14},{2,0},{4,2},{6,4},{8,6},{10,8},{12,10},{14,12},{1,15},{3,1}... | collective-permute-start | bytes 884744 | tf_op jit(solution)/shard_map/ring/ppermute | solution.py:26
  93.2 4.2 %collective-permute-done.14.up = bf16[384,384]{1,0:T(8,128)(2,1)S(1)} collective-permute-done((bf16[384,384]{1,0:T(8,128)(2,1)S(1)}, bf16[384,384]{1,0:T(8,128)(2,1)S(1)}, u32[]{:S(2)}, u32[]{:S(2)}) %collective-permute-start.14) | collective-permute-done | bytes 294944 | tf_op jit(solution)/shard_map/ring/ppermute | solution.py:26
  101.9 5.6 %collective-permute-done.19.refs_1_ = bf16[2,192,384]{2,1,0:T(8,128)(2,1)S(1)} collective-permute-done((bf16[2,192,384]{2,1,0:T(8,128)(2,1)S(1)}, bf16[2,192,384]{2,1,0:T(8,128)(2,1)S(1)}, u32[]{:S(2)}, u32[]{:S(2)}) %collective-permute-start.19) | collective-permute-done | bytes 294944 | tf_op jit(solution)/shard_map/combined/ppermute | solution.py:26
  107.4 3.5 %collective-permute-start.22 = (bf16[2,192,384]{2,1,0:T(8,128)(2,1)S(1)}, bf16[2,192,384]{2,1,0:T(8,128)(2,1)S(1)}, u32[]{:S(2)}, u32[]{:S(2)}) collective-permute-start(bf16[2,192,384]{2,1,0:T(8,128)(2,1)S(1)} %collective-permute-done.20.refs_2_), channel_id=1, source_target_pairs={{0,14},{2,0},{4,2},{6,4},{8,6},{10,8},{12,10},{14,12},{1,15},{3,1}... | collective-permute-start | bytes 884744 | tf_op jit(solution)/shard_map/combined/ppermute | solution.py:26
  110.9 6.8 %collective-permute-done.21.refs_3_ = bf16[2,192,384]{2,1,0:T(8,128)(2,1)S(1)} collective-permute-done((bf16[2,192,384]{2,1,0:T(8,128)(2,1)S(1)}, bf16[2,192,384]{2,1,0:T(8,128)(2,1)S(1)}, u32[]{:S(2)}, u32[]{:S(2)}) %collective-permute-start.21) | collective-permute-done | bytes 294944 | tf_op jit(solution)/shard_map/combined/ppermute | solution.py:26
  117.7 3.7 %collective-permute-start.24 = (bf16[2,192,384]{2,1,0:T(8,128)(2,1)S(1)}, bf16[2,192,384]{2,1,0:T(8,128)(2,1)S(1)}, u32[]{:S(2)}, u32[]{:S(2)}) collective-permute-start(bf16[2,192,384]{2,1,0:T(8,128)(2,1)S(1)} %collective-permute-done.22.refs_4_), channel_id=1, source_target_pairs={{0,14},{2,0},{4,2},{6,4},{8,6},{10,8},{12,10},{14,12},{1,15},{3,1}... | collective-permute-start | bytes 884744 | tf_op jit(solution)/shard_map/combined/ppermute | solution.py:26
  121.4 6.1 %collective-permute-done.23.refs_5_ = bf16[2,192,384]{2,1,0:T(8,128)(2,1)S(1)} collective-permute-done((bf16[2,192,384]{2,1,0:T(8,128)(2,1)S(1)}, bf16[2,192,384]{2,1,0:T(8,128)(2,1)S(1)}, u32[]{:S(2)}, u32[]{:S(2)}) %collective-permute-start.23) | collective-permute-done | bytes 294944 | tf_op jit(solution)/shard_map/combined/ppermute | solution.py:26
  133.7 6.2 %gamma.3 = (bf16[4,24,1792]{2,1,0:T(8,128)(2,1)S(1)}, bf16[4,24,1792]{2,1,0:T(8,128)(2,1)S(1)}, bf16[4,24,1792]{2,1,0:T(8,128)(2,1)S(1)}, f32[4,24,1792]{2,1,0:T(8,128)S(1)}) custom-call(bf16[2,192,384]{2,1,0:T(8,128)(2,1)S(1)} %combined.1.refs_0_, bf16[2,192,384]{2,1,0:T(8,128)(2,1)S(1)} %collective-permute-done.19.refs_1_, ...), custom_call_target="tpu_custom_call" | custom-call | tf_op jit(solution)/shard_map/gamma/pallas_call | solution.py:239
  143.6 6.2 %gamma.2 = (f32[4,24,1792]{2,1,0:T(8,128)S(1)}, f32[4,24,1792]{2,1,0:T(8,128)S(1)}, f32[4,24,1792]{2,1,0:T(8,128)S(1)}, bf16[4,24,1792]{2,1,0:T(8,128)(2,1)S(1)}) custom-call(bf16[2,192,384]{2,1,0:T(8,128)(2,1)S(1)} %combined.1.refs_0_, bf16[2,192,384]{2,1,0:T(8,128)(2,1)S(1)} %collective-permute-done.19.refs_1_, ...), custom_call_target="tpu_custom_call" | custom-call | tf_op jit(solution)/shard_map/gamma/pallas_call | solution.py:239
  155.9 4.0 %collective-permute-done.35 = bf16[4,24,1792]{2,1,0:T(8,128)(2,1)S(1)} collective-permute-done((bf16[4,24,1792]{2,1,0:T(8,128)(2,1)S(1)}, bf16[4,24,1792]{2,1,0:T(8,128)(2,1)S(1)}, u32[]{:S(2)}, u32[]{:S(2)}) %collective-permute-start.35) | collective-permute-done | bytes 344096 | tf_op jit(solution)/shard_map/gamma/ppermute | solution.py:21
  167.5 3.4 %collective-permute-start.38 = (bf16[24,1792]{1,0:T(8,128)(2,1)S(1)}, bf16[24,1792]{1,0:T(8,128)(2,1)S(1)}, u32[]{:S(2)}, u32[]{:S(2)}) collective-permute-start(bf16[24,1792]{1,0:T(8,128)(2,1)S(1)} %get-tuple-element.70), channel_id=1, source_target_pairs={{0,12},{2,14},{4,0},{6,2},{8,4},{10,6},{12,8},{14,10},{1,13},{3,15... | collective-permute-start | bytes 258056 | tf_op jit(solution)/shard_map/spread/ppermute | solution.py:26
  170.9 3.8 %collective-permute-start.39 = (bf16[24,1792]{1,0:T(8,128)(2,1)S(1)}, bf16[24,1792]{1,0:T(8,128)(2,1)S(1)}, u32[]{:S(2)}, u32[]{:S(2)}) collective-permute-start(bf16[24,1792]{1,0:T(8,128)(2,1)S(1)} %get-tuple-element.69), channel_id=1, source_target_pairs={{0,14},{2,0},{4,2},{6,4},{8,6},{10,8},{12,10},{14,12},{1,15},{3,1}... | collective-permute-start | bytes 258056 | tf_op jit(solution)/shard_map/spread/ppermute | solution.py:26
  181.6 4.8 %collective-permute-done.33.refs_3_ = bf16[24,1792]{1,0:T(8,128)(2,1)S(1)} collective-permute-done((bf16[24,1792]{1,0:T(8,128)(2,1)S(1)}, bf16[24,1792]{1,0:T(8,128)(2,1)S(1)}, u32[]{:S(2)}, u32[]{:S(2)}) %collective-permute-start.33) | collective-permute-done | bytes 86048 | tf_op jit(solution)/shard_map/spread/ppermute | solution.py:26
  (107 shorter events, 61.7 us)
Async XLA Ops:
  2.7 19.8 %collective-permute-start.5 = (bf16[384,896]{1,0:T(8,128)(2,1)S(1)}, bf16[384,896]{1,0:T(8,128)(2,1)S(1)}, u32[]{:S(2)}, u32[]{:S(2)}) collective-permute-start(bf16[384,896]{1,0:T(8,128)(2,1)S(1)} %bitcast.29), channel_id=1, source_target_pairs={{0,33},{1,32},{32,1},{33,0},{2,35},{3,34},{34,3},{35,2},{4,37},{5,... | collective-permute-start | bytes 2064392 | tf_op jit(solution)/shard_map/gather/ppermute | solution.py:21
  7.0 15.5 %collective-permute-start.3 = (bf16[384,896]{1,0:T(8,128)(2,1)S(1)}, bf16[384,896]{1,0:T(8,128)(2,1)S(1)}, u32[]{:S(2)}, u32[]{:S(2)}) collective-permute-start(bf16[384,896]{1,0:T(8,128)(2,1)S(1)} %collective-permute-done.refs_0_), channel_id=1, source_target_pairs={{0,64},{64,128},{128,192},{192,0},{1,65},{65,129},{129,193},{193,1... | collective-permute-start | bytes 2064392 | tf_op jit(solution)/shard_map/gather/ppermute | solution.py:26
  8.6 13.9 %collective-permute-start.4 = (bf16[384,896]{1,0:T(8,128)(2,1)S(1)}, bf16[384,896]{1,0:T(8,128)(2,1)S(1)}, u32[]{:S(2)}, u32[]{:S(2)}) collective-permute-start(bf16[384,896]{1,0:T(8,128)(2,1)S(1)} %collective-permute-done.refs_0_), channel_id=1, source_target_pairs={{0,192},{64,0},{128,64},{192,128},{1,193},{65,1},{129,65},{193,129... | collective-permute-start | bytes 2064392 | tf_op jit(solution)/shard_map/gather/ppermute | solution.py:26
  10.2 19.1 %collective-permute-start.2 = (bf16[384,896]{1,0:T(8,128)(2,1)S(1)}, bf16[384,896]{1,0:T(8,128)(2,1)S(1)}, u32[]{:S(2)}, u32[]{:S(2)}) collective-permute-start(bf16[384,896]{1,0:T(8,128)(2,1)S(1)} %bitcast.30), channel_id=1, source_target_pairs={{0,1},{17,16},{2,3},{19,18},{4,5},{21,20},{6,7},{23,22},{8,9},{25,... | collective-permute-start | bytes 2064392 | tf_op jit(solution)/shard_map/gather/ppermute | solution.py:174
  29.3 18.4 %collective-permute-start.8 = (bf16[384,896]{1,0:T(8,128)(2,1)S(1)}, bf16[384,896]{1,0:T(8,128)(2,1)S(1)}, u32[]{:S(2)}, u32[]{:S(2)}) collective-permute-start(bf16[384,896]{1,0:T(8,128)(2,1)S(1)} %bitcast.31), channel_id=1, source_target_pairs={{0,32},{1,33},{32,0},{33,1},{2,34},{3,35},{34,2},{35,3},{4,36},{5,... | collective-permute-start | bytes 2064392 | tf_op jit(solution)/shard_map/gather/ppermute | solution.py:21
  32.2 17.8 %collective-permute-start.9 = (bf16[768,896]{1,0:T(8,128)(2,1)S(1)}, bf16[768,896]{1,0:T(8,128)(2,1)S(1)}, u32[]{:S(2)}, u32[]{:S(2)}) collective-permute-start(bf16[768,896]{1,0:T(8,128)(2,1)S(1)} %constant_dynamic-update-slice_fusion.refs_1_), channel_id=1, source_target_pairs={{0,16},{16,0},{1,17},{17,1},{2,18},{18,2},{3,19},{19,3},{4,20},{20... | collective-permute-start | bytes 4128776 | tf_op jit(solution)/shard_map/gather/ppermute | solution.py:30
  32.4 11.7 %collective-permute-start.6 = (bf16[192,896]{1,0:T(8,128)(2,1)S(1)}, bf16[192,896]{1,0:T(8,128)(2,1)S(1)}, u32[]{:S(2)}, u32[]{:S(2)}) collective-permute-start(bf16[192,896]{1,0:T(8,128)(2,1)S(1)} %slice.36), channel_id=1, source_target_pairs={{0,64},{64,128},{128,192},{192,0},{1,65},{65,129},{129,193},{193,1... | collective-permute-start | bytes 1032200 | tf_op jit(solution)/shard_map/gather/ppermute | solution.py:26
  32.8 11.3 %collective-permute-start.7 = (bf16[192,896]{1,0:T(8,128)(2,1)S(1)}, bf16[192,896]{1,0:T(8,128)(2,1)S(1)}, u32[]{:S(2)}, u32[]{:S(2)}) collective-permute-start(bf16[192,896]{1,0:T(8,128)(2,1)S(1)} %slice.37), channel_id=1, source_target_pairs={{0,192},{64,0},{128,64},{192,128},{1,193},{65,1},{129,65},{193,129... | collective-permute-start | bytes 1032200 | tf_op jit(solution)/shard_map/gather/ppermute | solution.py:26
  61.2 9.7 %collective-permute-start.11 = (bf16[192,384]{1,0:T(8,128)(2,1)S(1)}, bf16[192,384]{1,0:T(8,128)(2,1)S(1)}, u32[]{:S(2)}, u32[]{:S(2)}) collective-permute-start(bf16[192,384]{1,0:T(8,128)(2,1)S(1)} %get-tuple-element.47), channel_id=1, source_target_pairs={{0,2},{2,4},{4,6},{6,8},{8,10},{10,12},{12,14},{14,0},{1,3},{3,5},... | collective-permute-start | bytes 442376 | tf_op jit(solution)/shard_map/ring/ppermute | solution.py:26
  67.3 9.1 %collective-permute-start.16 = (bf16[384,384]{1,0:T(8,128)(2,1)S(1)}, bf16[384,384]{1,0:T(8,128)(2,1)S(1)}, u32[]{:S(2)}, u32[]{:S(2)}) collective-permute-start(bf16[384,384]{1,0:T(8,128)(2,1)S(1)} %pad_maximum_fusion.1), channel_id=1, source_target_pairs={{0,14},{2,0},{4,2},{6,4},{8,6},{10,8},{12,10},{14,12},{1,15},{3,1}... | collective-permute-start | bytes 884744 | tf_op jit(solution)/shard_map/ring/ppermute | solution.py:26
  71.0 9.7 %collective-permute-start.12 = (bf16[384,384]{1,0:T(8,128)(2,1)S(1)}, bf16[384,384]{1,0:T(8,128)(2,1)S(1)}, u32[]{:S(2)}, u32[]{:S(2)}) collective-permute-start(bf16[384,384]{1,0:T(8,128)(2,1)S(1)} %pad_maximum_fusion), channel_id=1, source_target_pairs={{0,2},{2,4},{4,6},{6,8},{8,10},{10,12},{12,14},{14,0},{1,3},{3,5},... | collective-permute-start | bytes 884744 | tf_op jit(solution)/shard_map/ring/ppermute | solution.py:26
  98.5 9.0 %collective-permute-start.19 = (bf16[2,192,384]{2,1,0:T(8,128)(2,1)S(1)}, bf16[2,192,384]{2,1,0:T(8,128)(2,1)S(1)}, u32[]{:S(2)}, u32[]{:S(2)}) collective-permute-start(bf16[2,192,384]{2,1,0:T(8,128)(2,1)S(1)} %combined.1.refs_0_), channel_id=1, source_target_pairs={{0,2},{2,4},{4,6},{6,8},{8,10},{10,12},{12,14},{14,0},{1,3},{3,5},... | collective-permute-start | bytes 884744 | tf_op jit(solution)/shard_map/combined/ppermute | solution.py:26
  107.4 10.3 %collective-permute-start.21 = (bf16[2,192,384]{2,1,0:T(8,128)(2,1)S(1)}, bf16[2,192,384]{2,1,0:T(8,128)(2,1)S(1)}, u32[]{:S(2)}, u32[]{:S(2)}) collective-permute-start(bf16[2,192,384]{2,1,0:T(8,128)(2,1)S(1)} %collective-permute-done.19.refs_1_), channel_id=1, source_target_pairs={{0,2},{2,4},{4,6},{6,8},{8,10},{10,12},{12,14},{14,0},{1,3},{3,5},... | collective-permute-start | bytes 884744 | tf_op jit(solution)/shard_map/combined/ppermute | solution.py:26
  107.4 10.3 %collective-permute-start.22 = (bf16[2,192,384]{2,1,0:T(8,128)(2,1)S(1)}, bf16[2,192,384]{2,1,0:T(8,128)(2,1)S(1)}, u32[]{:S(2)}, u32[]{:S(2)}) collective-permute-start(bf16[2,192,384]{2,1,0:T(8,128)(2,1)S(1)} %collective-permute-done.20.refs_2_), channel_id=1, source_target_pairs={{0,14},{2,0},{4,2},{6,4},{8,6},{10,8},{12,10},{14,12},{1,15},{3,1}... | collective-permute-start | bytes 884744 | tf_op jit(solution)/shard_map/combined/ppermute | solution.py:26
  117.7 9.8 %collective-permute-start.23 = (bf16[2,192,384]{2,1,0:T(8,128)(2,1)S(1)}, bf16[2,192,384]{2,1,0:T(8,128)(2,1)S(1)}, u32[]{:S(2)}, u32[]{:S(2)}) collective-permute-start(bf16[2,192,384]{2,1,0:T(8,128)(2,1)S(1)} %collective-permute-done.21.refs_3_), channel_id=1, source_target_pairs={{0,2},{2,4},{4,6},{6,8},{8,10},{10,12},{12,14},{14,0},{1,3},{3,5},... | collective-permute-start | bytes 884744 | tf_op jit(solution)/shard_map/combined/ppermute | solution.py:26
  117.7 9.9 %collective-permute-start.24 = (bf16[2,192,384]{2,1,0:T(8,128)(2,1)S(1)}, bf16[2,192,384]{2,1,0:T(8,128)(2,1)S(1)}, u32[]{:S(2)}, u32[]{:S(2)}) collective-permute-start(bf16[2,192,384]{2,1,0:T(8,128)(2,1)S(1)} %collective-permute-done.22.refs_4_), channel_id=1, source_target_pairs={{0,14},{2,0},{4,2},{6,4},{8,6},{10,8},{12,10},{14,12},{1,15},{3,1}... | collective-permute-start | bytes 884744 | tf_op jit(solution)/shard_map/combined/ppermute | solution.py:26
  139.9 11.1 %collective-permute-start.27 = (bf16[4,24,1792]{2,1,0:T(8,128)(2,1)S(1)}, bf16[4,24,1792]{2,1,0:T(8,128)(2,1)S(1)}, u32[]{:S(2)}, u32[]{:S(2)}) collective-permute-start(bf16[4,24,1792]{2,1,0:T(8,128)(2,1)S(1)} %get-tuple-element.60), channel_id=1, source_target_pairs={{0,33},{1,32},{32,1},{33,0},{2,35},{3,34},{34,3},{35,2},{4,37},{5,... | collective-permute-start | bytes 1032200 | tf_op jit(solution)/shard_map/gamma/ppermute | solution.py:21
  141.3 9.7 %collective-permute-start.28 = (bf16[4,24,1792]{2,1,0:T(8,128)(2,1)S(1)}, bf16[4,24,1792]{2,1,0:T(8,128)(2,1)S(1)}, u32[]{:S(2)}, u32[]{:S(2)}) collective-permute-start(bf16[4,24,1792]{2,1,0:T(8,128)(2,1)S(1)} %get-tuple-element.61), channel_id=1, source_target_pairs={{0,1},{1,0},{32,33},{33,32},{2,3},{3,2},{34,35},{35,34},{4,5},{5,4... | collective-permute-start | bytes 1032200 | tf_op jit(solution)/shard_map/gamma/ppermute | solution.py:21
  142.9 28.0 %collective-permute-start.30 = (bf16[4,24,1792]{2,1,0:T(8,128)(2,1)S(1)}, bf16[4,24,1792]{2,1,0:T(8,128)(2,1)S(1)}, u32[]{:S(2)}, u32[]{:S(2)}) collective-permute-start(bf16[4,24,1792]{2,1,0:T(8,128)(2,1)S(1)} %get-tuple-element.64), channel_id=1, source_target_pairs={{0,33},{1,32},{32,1},{33,0},{2,35},{3,34},{34,3},{35,2},{4,37},{5,... | collective-permute-start | bytes 1032200 | tf_op jit(solution)/shard_map/gamma/ppermute | solution.py:21
  154.1 20.7 %collective-permute-start.29 = (bf16[4,24,1792]{2,1,0:T(8,128)(2,1)S(1)}, bf16[4,24,1792]{2,1,0:T(8,128)(2,1)S(1)}, u32[]{:S(2)}, u32[]{:S(2)}) collective-permute-start(bf16[4,24,1792]{2,1,0:T(8,128)(2,1)S(1)} %add_convert_fusion.3), channel_id=1, source_target_pairs={{0,1},{1,0},{32,33},{33,32},{2,3},{3,2},{34,35},{35,34},{4,5},{5,4... | collective-permute-start | bytes 1032200 | tf_op jit(solution)/shard_map/gamma/ppermute | solution.py:21
  161.1 13.8 %collective-permute-start.36 = (bf16[24,1792]{1,0:T(8,128)(2,1)S(1)}, bf16[24,1792]{1,0:T(8,128)(2,1)S(1)}, u32[]{:S(2)}, u32[]{:S(2)}) collective-permute-start(bf16[24,1792]{1,0:T(8,128)(2,1)S(1)} %get-tuple-element.72), channel_id=1, source_target_pairs={{0,8},{2,10},{4,12},{6,14},{8,0},{10,2},{12,4},{14,6},{1,9},{3,11}... | collective-permute-start | bytes 258056 | tf_op jit(solution)/shard_map/spread/ppermute | solution.py:26
  164.2 12.7 %collective-permute-start.37 = (bf16[24,1792]{1,0:T(8,128)(2,1)S(1)}, bf16[24,1792]{1,0:T(8,128)(2,1)S(1)}, u32[]{:S(2)}, u32[]{:S(2)}) collective-permute-start(bf16[24,1792]{1,0:T(8,128)(2,1)S(1)} %get-tuple-element.71), channel_id=1, source_target_pairs={{0,10},{2,12},{4,14},{6,0},{8,2},{10,4},{12,6},{14,8},{1,11},{3,13... | collective-permute-start | bytes 258056 | tf_op jit(solution)/shard_map/spread/ppermute | solution.py:26
  167.5 11.1 %collective-permute-start.38 = (bf16[24,1792]{1,0:T(8,128)(2,1)S(1)}, bf16[24,1792]{1,0:T(8,128)(2,1)S(1)}, u32[]{:S(2)}, u32[]{:S(2)}) collective-permute-start(bf16[24,1792]{1,0:T(8,128)(2,1)S(1)} %get-tuple-element.70), channel_id=1, source_target_pairs={{0,12},{2,14},{4,0},{6,2},{8,4},{10,6},{12,8},{14,10},{1,13},{3,15... | collective-permute-start | bytes 258056 | tf_op jit(solution)/shard_map/spread/ppermute | solution.py:26
  176.9 9.6 %collective-permute-start.33 = (bf16[24,1792]{1,0:T(8,128)(2,1)S(1)}, bf16[24,1792]{1,0:T(8,128)(2,1)S(1)}, u32[]{:S(2)}, u32[]{:S(2)}) collective-permute-start(bf16[24,1792]{1,0:T(8,128)(2,1)S(1)} %get-tuple-element.73), channel_id=1, source_target_pairs={{0,6},{2,8},{4,10},{6,12},{8,14},{10,0},{12,2},{14,4},{1,7},{3,9},... | collective-permute-start | bytes 258056 | tf_op jit(solution)/shard_map/spread/ppermute | solution.py:26
  (25 other events, 186.9 us)
where the time goes:
time: 188 us; the launch traced here: 187 us
  waiting for transfers between devices  80.6 us (43%)
  starting transfers between devices  77.9 us (41%)
  Pallas kernels  23.4 us (12%)
  local copies, waits for them, and re-layouts  2.58 us (1%)
  other arithmetic  2.53 us (1%)
    ppermute x27, waiting for transfers between devices, shift(): lax.ppermute(value, axis, [(i, (i + steps) % count) for i in range(count)])  60.4 us
    ppermute x27, starting transfers between devices, shift(): lax.ppermute(value, axis, [(i, (i + steps) % count) for i in range(count)])  50.7 us
    ppermute x8, starting transfers between devices, flip_x(): return lax.ppermute(value, X, [(i, i ^ bits) for i in range(NXH * NXL)])  15.5 us
    pallas_call x2, Pallas kernels, gamma_of(): pl.pallas_call(functools.partial(gamma_kernel, group=group), out_shape=[j...  12.4 us
    ppermute x8, waiting for transfers between devices, flip_x(): return lax.ppermute(value, X, [(i, i ^ bits) for i in range(NXH * NXL)])  11.2 us
    ppermute x1, starting transfers between devices, on_device(): xlf = lax.ppermute(own, ('core', 'xl'), [(0, 1), (3, 2)])  10.6 us
    pallas_call x1, Pallas kernels, on_device(): pl.pallas_call(coulomb_kernel, out_shape=[whole, whole, whole, part, part...  9.04 us
    ppermute x1, waiting for transfers between devices, on_device(): xlf = lax.ppermute(own, ('core', 'xl'), [(0, 1), (3, 2)])  6.82 us
  transfers between devices with their start and end apart: 40, of which 23 were waited for; matrix products, arithmetic and copies ran while one was open for 1% of the time, Pallas kernels for 3%

commit v1 on v0

--- a/solution.py
+++ b/solution.py
@@ -34,62 +34,93 @@
     return lax.dot_general(a, b, (((1,), (1,)), ((), ())), preferred_element_type=F32)
 
 
-def coulomb_kernel(own, xlf, bof, xh, *refs):
-    near, far, (p0, p1, p2, p3, p5, p6, p7), refs = refs[0:3], refs[3:6], refs[6:13], refs[13:]
-    send_up, send_down, keep_up, keep_down, stack_out, out, stack, left, sem = refs
-    z, xl, c = lax.axis_index("z"), lax.axis_index("xl"), lax.axis_index("core")
-    rows, half = own.shape
-
-    def lay(target, row0, col0, piece):
-        step = 64
-
-        def body(n, carry):
-            rows_at = pl.multiple_of(row0 + n * step, step)
-            target[pl.ds(rows_at, step), col0:col0 + half] = piece[pl.ds(pl.multiple_of(n * step, step), step), :]
-            return carry
-
-        lax.fori_loop(0, piece.shape[0] // step, body, 0)
-
+def lay(target, row0, col0, piece):
+    step, width = 64, piece.shape[1]
+
+    def body(n, carry):
+        rows_at = pl.multiple_of(row0 + n * step, step)
+        target[pl.ds(rows_at, step), col0:col0 + width] = piece[pl.ds(pl.multiple_of(n * step, step), step), :]
+        return carry
+
+    lax.fori_loop(0, piece.shape[0] // step, body, 0)
+
+
+def stacked(target, near, far):
     for k, pieces in enumerate((near, far)):
         at = 0
         for piece in pieces:
-            lay(stack, at, k * half, piece)
+            lay(target, at, k * piece.shape[1], piece)
             at += piece.shape[0]
-    copy = pltpu.make_async_copy(stack, stack_out, sem)
-    copy.start()
+
+
+def early_kernel(own, xlf, *refs):
+    near, far, (out, stack, left) = refs[0:3], refs[3:6], refs[6:9]
+    xl, c = lax.axis_index("xl"), lax.axis_index("core")
+    rows, half = own.shape
+    stacked(stack, near, far)
 
     @pl.when(xl == c)
     def _():
         lay(left, 0, 0, own)
         lay(left, 0, half, far[0])
-        lay(left, rows, 0, xh)
-        lay(left, rows, half, bof)
 
     @pl.when(xl != c)
     def _():
         lay(left, 0, half, own)
         lay(left, 0, 0, xlf)
-        lay(left, rows, half, xh)
-        lay(left, rows, 0, bof)
 
     def block(n, carry):
-        e, pair = n // 2, lax.rem(n, 2)
-        got = dot_t(
-            left[pl.ds(pl.multiple_of(e * rows, 128), rows), :],
-            stack[pl.ds(pl.multiple_of(pair * 2 * rows, 128), 2 * rows), :],
-        )
-        for dd in range(2):
-            out[lax.rem(e * NY + pair * 2 + dd + NZ - z, NZ)] = got[:, dd * rows:(dd + 1) * rows]
-        return carry
-
-    lax.fori_loop(0, NY, block, 0)
+        out[n] = dot_t(left[...], stack[pl.ds(pl.multiple_of(n * rows, 128), rows), :])
+        return carry
+
+    lax.fori_loop(0, NY - 1, block, 0)
+
+
+def coulomb_kernel(early, left, bof, xh, many, *refs):
+    near, far, (p0, p1, p2, p3, p5, p6, p7), refs = refs[0:2], refs[2:4], refs[4:11], refs[11:]
+    send_up, send_down, keep_up, keep_down, last, out, flipped = refs
+    z, xl, c = lax.axis_index("z"), lax.axis_index("xl"), lax.axis_index("core")
+    rows, half = bof.shape
+    stacked(last, near, far)
+
+    @pl.when(xl == c)
+    def _():
+        lay(flipped, 0, 0, xh)
+        lay(flipped, 0, half, bof)
+
+    @pl.when(xl != c)
+    def _():
+        lay(flipped, 0, half, xh)
+        lay(flipped, 0, 0, bof)
+
+    def place(e, d):
+        return lax.rem(e * NY + d + NZ - z, NZ)
+
+    def block(n, carry):
+        out[place(1, n)] = dot_t(flipped[...], many[pl.ds(pl.multiple_of(n * rows, 128), rows), :])
+        out[place(0, n)] = early[n]
+        return carry
+
+    lax.fori_loop(0, NY - 1, block, 0)
+
+    def end(e, carry):
+        @pl.when(e == 0)
+        def _():
+            out[place(0, NY - 1)] = dot_t(left[...], last[...])
+
+        @pl.when(e == 1)
+        def _():
+            out[place(1, NY - 1)] = dot_t(flipped[...], last[...])
+
+        return carry
+
+    lax.fori_loop(0, 2, end, 0)
     low, high = slice(0, rows // 2), slice(rows // 2, rows)
     for k, ref in ((0, p0), (1, p1), (2, p2), (6, p6), (7, p7)):
         ref[...] = out[k]
     p3[...], p5[...] = out[3, low, :], out[5, high, :]
     send_up[...], send_down[...] = out[4, low, :].astype(BF), out[4, high, :].astype(BF)
     keep_up[...], keep_down[...] = out[3, high, :].astype(BF), out[5, low, :].astype(BF)
-    copy.wait()
 
 
 def combined_kernel(occ_ref, v_col, v_row, mine, up, down, out, scr):
@@ -116,7 +147,7 @@
 
 
 def gamma_kernel(*refs, group):
-    combs, stack, outs, (left, scr) = refs[0:9], refs[9], refs[10:-2], refs[-2:]
+    combs, many, last, outs, (left, scr) = refs[0:9], refs[9], refs[10], refs[11:-2], refs[-2:]
     half, rows = combs[0].shape[1:]
     z, xl = lax.axis_index("z"), lax.axis_index("xl")
     part = combs[7].shape[1]
@@ -136,14 +167,15 @@
 
     def columns(n, carry):
         cols = pl.ds(pl.multiple_of(n * width, width), width)
-        acc = jnp.dot(left[...], stack[:, cols], preferred_element_type=F32)
+        acc = jnp.dot(left[:, :many.shape[0]], many[:, cols], preferred_element_type=F32)
+        acc += jnp.dot(left[:, many.shape[0]:], last[:, cols], preferred_element_type=F32)
         for zp in range(NZ):
             at = lax.rem(zp + NZ - z, NZ)
             scr[0, at, :, cols] = acc[zp * piece:(zp + 1) * piece]
             scr[1, at, :, cols] = acc[half + zp * piece:half + (zp + 1) * piece]
         return carry
 
-    lax.fori_loop(0, stack.shape[1] // width, columns, 0)
+    lax.fori_loop(0, many.shape[1] // width, columns, 0)
     n = NZ // 2
     for fl in range(2):
         for p in range(2):
@@ -178,12 +210,7 @@
         xh = flip_x(own_b, 2)
         j1, j3, bof = lax.optimization_barrier((j1, j3, bof))
         j2a, j2b = shift(j1[:hr], "y", 1), shift(j3[hr:], "y", -1)
-        j2a, j2b, xh = lax.optimization_barrier((j2a, j2b, xh))
-        outer = jnp.concatenate([j1, j3])
-        outer_far = flip_core(outer)
-        inner = jnp.concatenate([j2a, j2b])
-        inner_far = flip_core(inner)
-        near, far = [j0, outer, inner], [f0, outer_far, inner_far]
+        f1, f3 = flip_core(j1), flip_core(j3)
 
     vmem = pl.BlockSpec(memory_space=pltpu.VMEM)
     smem = pl.BlockSpec(memory_space=pltpu.SMEM)
@@ -192,20 +219,28 @@
     with jax.named_scope("coulomb"):
         whole, part = jax.ShapeDtypeStruct((rows, rows), F32), jax.ShapeDtypeStruct((hr, rows), F32)
         sent = jax.ShapeDtypeStruct((hr, rows), BF)
-        mine, p1, p2, p3, p5, p6, p7, up, down, keep_up, keep_down, stack = pl.pallas_call(
+        early, many, left = pl.pallas_call(
+            early_kernel,
+            out_shape=[
+                jax.ShapeDtypeStruct((NY - 1, rows, rows), F32),
+                jax.ShapeDtypeStruct(((NY - 1) * rows, 2 * aux), BF),
+                jax.ShapeDtypeStruct((rows, 2 * aux), BF),
+            ],
+            in_specs=[vmem] * 8,
+            out_specs=[vmem] * 3,
+            compiler_params=params,
+        )(own, xlf, j0, j1, j3, f0, f1, f3)
+        early, j2a, j2b, xh = lax.optimization_barrier((early, j2a, j2b, xh))
+        f2a, f2b = flip_core(j2a), flip_core(j2b)
+        mine, p1, p2, p3, p5, p6, p7, up, down, keep_up, keep_down, last = pl.pallas_call(
             coulomb_kernel,
             out_shape=[whole, whole, whole, part, part, whole, whole, sent, sent, sent, sent]
-            + [jax.ShapeDtypeStruct((NY * rows, 2 * aux), BF)],
-            in_specs=[vmem] * 10,
-            out_specs=[vmem] * 11 + [pl.BlockSpec(memory_space=pl.ANY)],
-            scratch_shapes=[
-                pltpu.VMEM((NZ, rows, rows), F32),
-                pltpu.VMEM((NY * rows, 2 * aux), BF),
-                pltpu.VMEM((2 * rows, 2 * aux), BF),
-                pltpu.SemaphoreType.DMA,
-            ],
+            + [jax.ShapeDtypeStruct((rows, 2 * aux), BF)],
+            in_specs=[vmem] * 9,
+            out_specs=[vmem] * 12,
+            scratch_shapes=[pltpu.VMEM((NZ, rows, rows), F32), pltpu.VMEM((rows, 2 * aux), BF)],
             compiler_params=params,
-        )(own, xlf, bof, xh, *near, *far)
+        )(early, left, bof, xh, many, j2a, j2b, f2a, f2b)
 
     with jax.named_scope("ring"):
         up, down = shift(up, "z", 1), shift(down, "z", -1)
@@ -239,14 +274,14 @@
             return pl.pallas_call(
                 functools.partial(gamma_kernel, group=group),
                 out_shape=[jax.ShapeDtypeStruct((NZ // 2, piece, 2 * aux), t) for t in types],
-                in_specs=[vmem] * 10,
+                in_specs=[vmem] * 11,
                 out_specs=[vmem] * 4,
                 scratch_shapes=[
                     pltpu.VMEM((2 * hr, NY * rows), BF),
                     pltpu.VMEM((2, NZ, piece, 2 * aux), F32),
                 ],
                 compiler_params=params,
-            )(*combs, stack)
+            )(*combs, many, last)
 
         to_xh0, to_xh1, to_both0, to_both1 = gamma_of(1, (BF, BF, BF, F32))
         via_both, via_xl = flip_x(to_xh0, 3), flip_x(to_xh1, 1)

time: 188 us -> 186 us (0.989)
  waiting for transfers between devices: 80.6 us -> 71.3 us
  Pallas kernels: 23.4 us -> 28.8 us
  starting transfers between devices: 77.9 us -> 82.2 us
  local copies, waits for them, and re-layouts: 2.58 us -> 0.36 us
    ppermute x27, waiting for transfers between devices: 60.4 us -> 54.3 us  [shift(): lax.ppermute(value, axis, [(i, (i + steps) % count) for i in range(count)])]
    pallas_call x0 -> x1, Pallas kernels: none -> 5.29 us  [on_device(): pl.pallas_call(early_kernel, out_shape=[jax.ShapeDtypeStruct((NY - 1, row...]
    ppermute x3 -> x5, starting transfers between devices: 0.28 us -> 4.84 us  [flip_core(): return lax.ppermute(value, 'core', [(0, 1), (1, 0)])]
    ppermute x1, waiting for transfers between devices: 6.82 us -> 2.58 us  [on_device(): xlf = lax.ppermute(own, ('core', 'xl'), [(0, 1), (3, 2)])]
    unnamed x23 -> x11, local copies, waits for them, and re-layouts: 2.2 us -> 0.1 us
  transfers between devices with their start and end apart: 40 -> 42, of which waited for: 23 -> 25; matrix products, arithmetic and copies ran while one was open for 1% -> 1% of each run, Pallas kernels for 3% -> 6%
where the time goes in v1:
time: 186 us; the launch traced here: 185 us
  starting transfers between devices  82.2 us (44%)
  waiting for transfers between devices  71.3 us (38%)
  Pallas kernels  28.8 us (15%)
  other arithmetic  2.53 us (1%)
    ppermute x27, waiting for transfers between devices, shift(): lax.ppermute(value, axis, [(i, (i + steps) % count) for i in range(count)])  54.3 us
    ppermute x27, starting transfers between devices, shift(): lax.ppermute(value, axis, [(i, (i + steps) % count) for i in range(count)])  50.6 us
    ppermute x8, starting transfers between devices, flip_x(): return lax.ppermute(value, X, [(i, i ^ bits) for i in range(NXH * NXL)])  15.4 us
    ppermute x8, waiting for transfers between devices, flip_x(): return lax.ppermute(value, X, [(i, i ^ bits) for i in range(NXH * NXL)])  12.8 us
    pallas_call x2, Pallas kernels, gamma_of(): pl.pallas_call(functools.partial(gamma_kernel, group=group), out_shape=[j...  12.1 us
    ppermute x1, starting transfers between devices, on_device(): xlf = lax.ppermute(own, ('core', 'xl'), [(0, 1), (3, 2)])  10.6 us
    pallas_call x1, Pallas kernels, on_device(): pl.pallas_call(coulomb_kernel, out_shape=[whole, whole, whole, part, part...  9.44 us
    pallas_call x1, Pallas kernels, on_device(): pl.pallas_call(early_kernel, out_shape=[jax.ShapeDtypeStruct((NY - 1, row...  5.29 us
  transfers between devices with their start and end apart: 42, of which 25 were waited for; matrix products, arithmetic and copies ran while one was open for 1% of the time, Pallas kernels for 6%

profile of v1, /device:TPU:32, one launch (start us, length us, event | category | flops | bytes accessed | tf_op | source)
XLA Modules:
  0.0 185.4 jit_solution(13360452537899379339)
XLA Ops:
  2.7 4.3 %collective-permute-start.5 = (bf16[384,896]{1,0:T(8,128)(2,1)S(1)}, bf16[384,896]{1,0:T(8,128)(2,1)S(1)}, u32[]{:S(2)}, u32[]{:S(2)}) collective-permute-start(bf16[384,896]{1,0:T(8,128)(2,1)S(1)} %bitcast.29), channel_id=1, source_target_pairs={{0,33},{1,32},{32,1},{33,0},{2,35},{3,34},{34,3},{35,2},{4,37},{5,... | collective-permute-start | bytes 2064392 | tf_op jit(solution)/shard_map/gather/ppermute | solution.py:21
  10.2 10.6 %collective-permute-start.2 = (bf16[384,896]{1,0:T(8,128)(2,1)S(1)}, bf16[384,896]{1,0:T(8,128)(2,1)S(1)}, u32[]{:S(2)}, u32[]{:S(2)}) collective-permute-start(bf16[384,896]{1,0:T(8,128)(2,1)S(1)} %bitcast.30), channel_id=1, source_target_pairs={{0,1},{17,16},{2,3},{19,18},{4,5},{21,20},{6,7},{23,22},{8,9},{25,... | collective-permute-start | bytes 2064392 | tf_op jit(solution)/shard_map/gather/ppermute | solution.py:206
  22.5 4.2 %collective-permute-start.6 = (bf16[384,896]{1,0:T(8,128)(2,1)S(1)}, bf16[384,896]{1,0:T(8,128)(2,1)S(1)}, u32[]{:S(2)}, u32[]{:S(2)}) collective-permute-start(bf16[384,896]{1,0:T(8,128)(2,1)S(1)} %collective-permute-done.3.refs_1_), channel_id=1, source_target_pairs={{0,16},{16,0},{1,17},{17,1},{2,18},{18,2},{3,19},{19,3},{4,20},{20... | collective-permute-start | bytes 2064392 | tf_op jit(solution)/shard_map/gather/ppermute | solution.py:30
  35.4 5.3 %coulomb.2 = (f32[3,384,384]{2,1,0:T(8,128)}, bf16[1152,1792]{1,0:T(8,128)(2,1)}, bf16[384,1792]{1,0:T(8,128)(2,1)}) custom-call(bf16[384,896]{1,0:T(8,128)(2,1)S(1)} %bitcast.32, bf16[384,896]{1,0:T(8,128)(2,1)S(1)} %collective-permute-done.2.xlf, bf16[384,896]{1,0:T(8,128)(2,1)S(1)} %collective-permute-done.refs_0_, ...), custom_call_target="tpu_custom_call" | custom-call | tf_op jit(solution)/shard_map/coulomb/pallas_call | solution.py:222
  42.8 4.8 %collective-permute-done.10.xh = bf16[384,896]{1,0:T(8,128)(2,1)S(1)} collective-permute-done((bf16[384,896]{1,0:T(8,128)(2,1)S(1)}, bf16[384,896]{1,0:T(8,128)(2,1)S(1)}, u32[]{:S(2)}, u32[]{:S(2)}) %collective-permute-start.10) | collective-permute-done | bytes 688160 | tf_op jit(solution)/shard_map/gather/ppermute | solution.py:21
  49.8 9.4 %coulomb.3 = (f32[384,384]{1,0:T(8,128)S(1)}, f32[384,384]{1,0:T(8,128)S(1)}, f32[384,384]{1,0:T(8,128)S(1)}, f32[192,384]{1,0:T(8,128)S(1)}, f32[192,384]{1,0:T...) custom-call(f32[3,384,384]{2,1,0:T(8,128)} %get-tuple-element.47.ear, ...), custom_call_target="tpu_custom_call" | custom-call | tf_op jit(solution)/shard_map/coulomb/pallas_call | solution.py:235
  61.2 4.0 %collective-permute-done.17 = bf16[192,384]{1,0:T(8,128)(2,1)S(1)} collective-permute-done((bf16[192,384]{1,0:T(8,128)(2,1)S(1)}, bf16[192,384]{1,0:T(8,128)(2,1)S(1)}, u32[]{:S(2)}, u32[]{:S(2)}) %collective-permute-start.17) | collective-permute-done | bytes 147488 | tf_op jit(solution)/shard_map/ring/ppermute | solution.py:26
  65.4 3.6 %collective-permute-start.18 = (bf16[384,384]{1,0:T(8,128)(2,1)S(1)}, bf16[384,384]{1,0:T(8,128)(2,1)S(1)}, u32[]{:S(2)}, u32[]{:S(2)}) collective-permute-start(bf16[384,384]{1,0:T(8,128)(2,1)S(1)} %pad_maximum_fusion.1), channel_id=1, source_target_pairs={{0,14},{2,0},{4,2},{6,4},{8,6},{10,8},{12,10},{14,12},{1,15},{3,1}... | collective-permute-start | bytes 884744 | tf_op jit(solution)/shard_map/ring/ppermute | solution.py:26
  69.2 5.5 %collective-permute-done.18 = bf16[384,384]{1,0:T(8,128)(2,1)S(1)} collective-permute-done((bf16[384,384]{1,0:T(8,128)(2,1)S(1)}, bf16[384,384]{1,0:T(8,128)(2,1)S(1)}, u32[]{:S(2)}, u32[]{:S(2)}) %collective-permute-start.18) | collective-permute-done | bytes 294944 | tf_op jit(solution)/shard_map/ring/ppermute | solution.py:26
  74.7 3.8 %collective-permute-start.19 = (bf16[384,384]{1,0:T(8,128)(2,1)S(1)}, bf16[384,384]{1,0:T(8,128)(2,1)S(1)}, u32[]{:S(2)}, u32[]{:S(2)}) collective-permute-start(bf16[384,384]{1,0:T(8,128)(2,1)S(1)} %add_convert_fusion.5), channel_id=1, source_target_pairs={{0,14},{2,0},{4,2},{6,4},{8,6},{10,8},{12,10},{14,12},{1,15},{3,1}... | collective-permute-start | bytes 884744 | tf_op jit(solution)/shard_map/ring/ppermute | solution.py:26
  79.1 4.4 %collective-permute-done.19 = bf16[384,384]{1,0:T(8,128)(2,1)S(1)} collective-permute-done((bf16[384,384]{1,0:T(8,128)(2,1)S(1)}, bf16[384,384]{1,0:T(8,128)(2,1)S(1)}, u32[]{:S(2)}, u32[]{:S(2)}) %collective-permute-start.19) | collective-permute-done | bytes 294944 | tf_op jit(solution)/shard_map/ring/ppermute | solution.py:26
  83.6 3.5 %collective-permute-start.20 = (bf16[384,384]{1,0:T(8,128)(2,1)S(1)}, bf16[384,384]{1,0:T(8,128)(2,1)S(1)}, u32[]{:S(2)}, u32[]{:S(2)}) collective-permute-start(bf16[384,384]{1,0:T(8,128)(2,1)S(1)} %add_convert_fusion.4), channel_id=1, source_target_pairs={{0,14},{2,0},{4,2},{6,4},{8,6},{10,8},{12,10},{14,12},{1,15},{3,1}... | collective-permute-start | bytes 884744 | tf_op jit(solution)/shard_map/ring/ppermute | solution.py:26
  87.9 3.5 %collective-permute-done.20.down = bf16[384,384]{1,0:T(8,128)(2,1)S(1)} collective-permute-done((bf16[384,384]{1,0:T(8,128)(2,1)S(1)}, bf16[384,384]{1,0:T(8,128)(2,1)S(1)}, u32[]{:S(2)}, u32[]{:S(2)}) %collective-permute-start.20) | collective-permute-done | bytes 294944 | tf_op jit(solution)/shard_map/ring/ppermute | solution.py:26
  91.4 4.3 %collective-permute-done.16.up = bf16[384,384]{1,0:T(8,128)(2,1)S(1)} collective-permute-done((bf16[384,384]{1,0:T(8,128)(2,1)S(1)}, bf16[384,384]{1,0:T(8,128)(2,1)S(1)}, u32[]{:S(2)}, u32[]{:S(2)}) %collective-permute-start.16) | collective-permute-done | bytes 294944 | tf_op jit(solution)/shard_map/ring/ppermute | solution.py:26
  100.1 5.6 %collective-permute-done.21.refs_1_ = bf16[2,192,384]{2,1,0:T(8,128)(2,1)S(1)} collective-permute-done((bf16[2,192,384]{2,1,0:T(8,128)(2,1)S(1)}, bf16[2,192,384]{2,1,0:T(8,128)(2,1)S(1)}, u32[]{:S(2)}, u32[]{:S(2)}) %collective-permute-start.21) | collective-permute-done | bytes 294944 | tf_op jit(solution)/shard_map/combined/ppermute | solution.py:26
  105.7 3.5 %collective-permute-start.24 = (bf16[2,192,384]{2,1,0:T(8,128)(2,1)S(1)}, bf16[2,192,384]{2,1,0:T(8,128)(2,1)S(1)}, u32[]{:S(2)}, u32[]{:S(2)}) collective-permute-start(bf16[2,192,384]{2,1,0:T(8,128)(2,1)S(1)} %collective-permute-done.22.refs_2_), channel_id=1, source_target_pairs={{0,14},{2,0},{4,2},{6,4},{8,6},{10,8},{12,10},{14,12},{1,15},{3,1}... | collective-permute-start | bytes 884744 | tf_op jit(solution)/shard_map/combined/ppermute | solution.py:26
  109.2 6.8 %collective-permute-done.23.refs_3_ = bf16[2,192,384]{2,1,0:T(8,128)(2,1)S(1)} collective-permute-done((bf16[2,192,384]{2,1,0:T(8,128)(2,1)S(1)}, bf16[2,192,384]{2,1,0:T(8,128)(2,1)S(1)}, u32[]{:S(2)}, u32[]{:S(2)}) %collective-permute-start.23) | collective-permute-done | bytes 294944 | tf_op jit(solution)/shard_map/combined/ppermute | solution.py:26
  116.0 3.7 %collective-permute-start.26 = (bf16[2,192,384]{2,1,0:T(8,128)(2,1)S(1)}, bf16[2,192,384]{2,1,0:T(8,128)(2,1)S(1)}, u32[]{:S(2)}, u32[]{:S(2)}) collective-permute-start(bf16[2,192,384]{2,1,0:T(8,128)(2,1)S(1)} %collective-permute-done.24.refs_4_), channel_id=1, source_target_pairs={{0,14},{2,0},{4,2},{6,4},{8,6},{10,8},{12,10},{14,12},{1,15},{3,1}... | collective-permute-start | bytes 884744 | tf_op jit(solution)/shard_map/combined/ppermute | solution.py:26
  119.7 6.1 %collective-permute-done.25.refs_5_ = bf16[2,192,384]{2,1,0:T(8,128)(2,1)S(1)} collective-permute-done((bf16[2,192,384]{2,1,0:T(8,128)(2,1)S(1)}, bf16[2,192,384]{2,1,0:T(8,128)(2,1)S(1)}, u32[]{:S(2)}, u32[]{:S(2)}) %collective-permute-start.25) | collective-permute-done | bytes 294944 | tf_op jit(solution)/shard_map/combined/ppermute | solution.py:26
  132.0 6.0 %gamma.3 = (bf16[4,24,1792]{2,1,0:T(8,128)(2,1)S(1)}, bf16[4,24,1792]{2,1,0:T(8,128)(2,1)S(1)}, bf16[4,24,1792]{2,1,0:T(8,128)(2,1)S(1)}, f32[4,24,1792]{2,1,0:T(8,128)S(1)}) custom-call(bf16[2,192,384]{2,1,0:T(8,128)(2,1)S(1)} %combined.1.refs_0_, bf16[2,192,384]{2,1,0:T(8,128)(2,1)S(1)} %collective-permute-done.21.refs_1_, ...), custom_call_target="tpu_custom_call" | custom-call | tf_op jit(solution)/shard_map/gamma/pallas_call | solution.py:274
  142.0 6.1 %gamma.2 = (f32[4,24,1792]{2,1,0:T(8,128)S(1)}, f32[4,24,1792]{2,1,0:T(8,128)S(1)}, f32[4,24,1792]{2,1,0:T(8,128)S(1)}, bf16[4,24,1792]{2,1,0:T(8,128)(2,1)S(1)}) custom-call(bf16[2,192,384]{2,1,0:T(8,128)(2,1)S(1)} %combined.1.refs_0_, bf16[2,192,384]{2,1,0:T(8,128)(2,1)S(1)} %collective-permute-done.21.refs_1_, ...), custom_call_target="tpu_custom_call" | custom-call | tf_op jit(solution)/shard_map/gamma/pallas_call | solution.py:274
  154.0 4.1 %collective-permute-done.37 = bf16[4,24,1792]{2,1,0:T(8,128)(2,1)S(1)} collective-permute-done((bf16[4,24,1792]{2,1,0:T(8,128)(2,1)S(1)}, bf16[4,24,1792]{2,1,0:T(8,128)(2,1)S(1)}, u32[]{:S(2)}, u32[]{:S(2)}) %collective-permute-start.37) | collective-permute-done | bytes 344096 | tf_op jit(solution)/shard_map/gamma/ppermute | solution.py:21
  169.0 3.6 %collective-permute-start.41 = (bf16[24,1792]{1,0:T(8,128)(2,1)S(1)}, bf16[24,1792]{1,0:T(8,128)(2,1)S(1)}, u32[]{:S(2)}, u32[]{:S(2)}) collective-permute-start(bf16[24,1792]{1,0:T(8,128)(2,1)S(1)} %get-tuple-element.77), channel_id=1, source_target_pairs={{0,14},{2,0},{4,2},{6,4},{8,6},{10,8},{12,10},{14,12},{1,15},{3,1}... | collective-permute-start | bytes 258056 | tf_op jit(solution)/shard_map/spread/ppermute | solution.py:26
  179.6 5.0 %collective-permute-done.35.refs_3_ = bf16[24,1792]{1,0:T(8,128)(2,1)S(1)} collective-permute-done((bf16[24,1792]{1,0:T(8,128)(2,1)S(1)}, bf16[24,1792]{1,0:T(8,128)(2,1)S(1)}, u32[]{:S(2)}, u32[]{:S(2)}) %collective-permute-start.35) | collective-permute-done | bytes 86048 | tf_op jit(solution)/shard_map/spread/ppermute | solution.py:26
  (98 shorter events, 63.4 us)
Async XLA Ops:
  2.7 19.8 %collective-permute-start.5 = (bf16[384,896]{1,0:T(8,128)(2,1)S(1)}, bf16[384,896]{1,0:T(8,128)(2,1)S(1)}, u32[]{:S(2)}, u32[]{:S(2)}) collective-permute-start(bf16[384,896]{1,0:T(8,128)(2,1)S(1)} %bitcast.29), channel_id=1, source_target_pairs={{0,33},{1,32},{32,1},{33,0},{2,35},{3,34},{34,3},{35,2},{4,37},{5,... | collective-permute-start | bytes 2064392 | tf_op jit(solution)/shard_map/gather/ppermute | solution.py:21
  7.0 15.5 %collective-permute-start.3 = (bf16[384,896]{1,0:T(8,128)(2,1)S(1)}, bf16[384,896]{1,0:T(8,128)(2,1)S(1)}, u32[]{:S(2)}, u32[]{:S(2)}) collective-permute-start(bf16[384,896]{1,0:T(8,128)(2,1)S(1)} %collective-permute-done.refs_0_), channel_id=1, source_target_pairs={{0,64},{64,128},{128,192},{192,0},{1,65},{65,129},{129,193},{193,1... | collective-permute-start | bytes 2064392 | tf_op jit(solution)/shard_map/gather/ppermute | solution.py:26
  8.6 13.9 %collective-permute-start.4 = (bf16[384,896]{1,0:T(8,128)(2,1)S(1)}, bf16[384,896]{1,0:T(8,128)(2,1)S(1)}, u32[]{:S(2)}, u32[]{:S(2)}) collective-permute-start(bf16[384,896]{1,0:T(8,128)(2,1)S(1)} %collective-permute-done.refs_0_), channel_id=1, source_target_pairs={{0,192},{64,0},{128,64},{192,128},{1,193},{65,1},{129,65},{193,129... | collective-permute-start | bytes 2064392 | tf_op jit(solution)/shard_map/gather/ppermute | solution.py:26
  10.2 19.1 %collective-permute-start.2 = (bf16[384,896]{1,0:T(8,128)(2,1)S(1)}, bf16[384,896]{1,0:T(8,128)(2,1)S(1)}, u32[]{:S(2)}, u32[]{:S(2)}) collective-permute-start(bf16[384,896]{1,0:T(8,128)(2,1)S(1)} %bitcast.30), channel_id=1, source_target_pairs={{0,1},{17,16},{2,3},{19,18},{4,5},{21,20},{6,7},{23,22},{8,9},{25,... | collective-permute-start | bytes 2064392 | tf_op jit(solution)/shard_map/gather/ppermute | solution.py:206
  22.5 12.9 %collective-permute-start.6 = (bf16[384,896]{1,0:T(8,128)(2,1)S(1)}, bf16[384,896]{1,0:T(8,128)(2,1)S(1)}, u32[]{:S(2)}, u32[]{:S(2)}) collective-permute-start(bf16[384,896]{1,0:T(8,128)(2,1)S(1)} %collective-permute-done.3.refs_1_), channel_id=1, source_target_pairs={{0,16},{16,0},{1,17},{17,1},{2,18},{18,2},{3,19},{19,3},{4,20},{20... | collective-permute-start | bytes 2064392 | tf_op jit(solution)/shard_map/gather/ppermute | solution.py:30
  29.3 18.4 %collective-permute-start.10 = (bf16[384,896]{1,0:T(8,128)(2,1)S(1)}, bf16[384,896]{1,0:T(8,128)(2,1)S(1)}, u32[]{:S(2)}, u32[]{:S(2)}) collective-permute-start(bf16[384,896]{1,0:T(8,128)(2,1)S(1)} %bitcast.31), channel_id=1, source_target_pairs={{0,32},{1,33},{32,0},{33,1},{2,34},{3,35},{34,2},{35,3},{4,36},{5,... | collective-permute-start | bytes 2064392 | tf_op jit(solution)/shard_map/gather/ppermute | solution.py:21
  32.1 10.7 %collective-permute-start.8 = (bf16[192,896]{1,0:T(8,128)(2,1)S(1)}, bf16[192,896]{1,0:T(8,128)(2,1)S(1)}, u32[]{:S(2)}, u32[]{:S(2)}) collective-permute-start(bf16[192,896]{1,0:T(8,128)(2,1)S(1)} %slice.36), channel_id=1, source_target_pairs={{0,64},{64,128},{128,192},{192,0},{1,65},{65,129},{129,193},{193,1... | collective-permute-start | bytes 1032200 | tf_op jit(solution)/shard_map/gather/ppermute | solution.py:26
  32.5 10.3 %collective-permute-start.9 = (bf16[192,896]{1,0:T(8,128)(2,1)S(1)}, bf16[192,896]{1,0:T(8,128)(2,1)S(1)}, u32[]{:S(2)}, u32[]{:S(2)}) collective-permute-start(bf16[192,896]{1,0:T(8,128)(2,1)S(1)} %slice.37), channel_id=1, source_target_pairs={{0,192},{64,0},{128,64},{192,128},{1,193},{65,1},{129,65},{193,129... | collective-permute-start | bytes 1032200 | tf_op jit(solution)/shard_map/gather/ppermute | solution.py:26
  59.3 9.7 %collective-permute-start.13 = (bf16[192,384]{1,0:T(8,128)(2,1)S(1)}, bf16[192,384]{1,0:T(8,128)(2,1)S(1)}, u32[]{:S(2)}, u32[]{:S(2)}) collective-permute-start(bf16[192,384]{1,0:T(8,128)(2,1)S(1)} %get-tuple-element.55), channel_id=1, source_target_pairs={{0,2},{2,4},{4,6},{6,8},{8,10},{10,12},{12,14},{14,0},{1,3},{3,5},... | collective-permute-start | bytes 442376 | tf_op jit(solution)/shard_map/ring/ppermute | solution.py:26
  65.4 9.3 %collective-permute-start.18 = (bf16[384,384]{1,0:T(8,128)(2,1)S(1)}, bf16[384,384]{1,0:T(8,128)(2,1)S(1)}, u32[]{:S(2)}, u32[]{:S(2)}) collective-permute-start(bf16[384,384]{1,0:T(8,128)(2,1)S(1)} %pad_maximum_fusion.1), channel_id=1, source_target_pairs={{0,14},{2,0},{4,2},{6,4},{8,6},{10,8},{12,10},{14,12},{1,15},{3,1}... | collective-permute-start | bytes 884744 | tf_op jit(solution)/shard_map/ring/ppermute | solution.py:26
  69.1 9.8 %collective-permute-start.14 = (bf16[384,384]{1,0:T(8,128)(2,1)S(1)}, bf16[384,384]{1,0:T(8,128)(2,1)S(1)}, u32[]{:S(2)}, u32[]{:S(2)}) collective-permute-start(bf16[384,384]{1,0:T(8,128)(2,1)S(1)} %pad_maximum_fusion), channel_id=1, source_target_pairs={{0,2},{2,4},{4,6},{6,8},{8,10},{10,12},{12,14},{14,0},{1,3},{3,5},... | collective-permute-start | bytes 884744 | tf_op jit(solution)/shard_map/ring/ppermute | solution.py:26
  96.7 9.0 %collective-permute-start.21 = (bf16[2,192,384]{2,1,0:T(8,128)(2,1)S(1)}, bf16[2,192,384]{2,1,0:T(8,128)(2,1)S(1)}, u32[]{:S(2)}, u32[]{:S(2)}) collective-permute-start(bf16[2,192,384]{2,1,0:T(8,128)(2,1)S(1)} %combined.1.refs_0_), channel_id=1, source_target_pairs={{0,2},{2,4},{4,6},{6,8},{8,10},{10,12},{12,14},{14,0},{1,3},{3,5},... | collective-permute-start | bytes 884744 | tf_op jit(solution)/shard_map/combined/ppermute | solution.py:26
  105.7 10.3 %collective-permute-start.23 = (bf16[2,192,384]{2,1,0:T(8,128)(2,1)S(1)}, bf16[2,192,384]{2,1,0:T(8,128)(2,1)S(1)}, u32[]{:S(2)}, u32[]{:S(2)}) collective-permute-start(bf16[2,192,384]{2,1,0:T(8,128)(2,1)S(1)} %collective-permute-done.21.refs_1_), channel_id=1, source_target_pairs={{0,2},{2,4},{4,6},{6,8},{8,10},{10,12},{12,14},{14,0},{1,3},{3,5},... | collective-permute-start | bytes 884744 | tf_op jit(solution)/shard_map/combined/ppermute | solution.py:26
  105.7 10.3 %collective-permute-start.24 = (bf16[2,192,384]{2,1,0:T(8,128)(2,1)S(1)}, bf16[2,192,384]{2,1,0:T(8,128)(2,1)S(1)}, u32[]{:S(2)}, u32[]{:S(2)}) collective-permute-start(bf16[2,192,384]{2,1,0:T(8,128)(2,1)S(1)} %collective-permute-done.22.refs_2_), channel_id=1, source_target_pairs={{0,14},{2,0},{4,2},{6,4},{8,6},{10,8},{12,10},{14,12},{1,15},{3,1}... | collective-permute-start | bytes 884744 | tf_op jit(solution)/shard_map/combined/ppermute | solution.py:26
  116.0 9.8 %collective-permute-start.25 = (bf16[2,192,384]{2,1,0:T(8,128)(2,1)S(1)}, bf16[2,192,384]{2,1,0:T(8,128)(2,1)S(1)}, u32[]{:S(2)}, u32[]{:S(2)}) collective-permute-start(bf16[2,192,384]{2,1,0:T(8,128)(2,1)S(1)} %collective-permute-done.23.refs_3_), channel_id=1, source_target_pairs={{0,2},{2,4},{4,6},{6,8},{8,10},{10,12},{12,14},{14,0},{1,3},{3,5},... | collective-permute-start | bytes 884744 | tf_op jit(solution)/shard_map/combined/ppermute | solution.py:26
  116.0 9.9 %collective-permute-start.26 = (bf16[2,192,384]{2,1,0:T(8,128)(2,1)S(1)}, bf16[2,192,384]{2,1,0:T(8,128)(2,1)S(1)}, u32[]{:S(2)}, u32[]{:S(2)}) collective-permute-start(bf16[2,192,384]{2,1,0:T(8,128)(2,1)S(1)} %collective-permute-done.24.refs_4_), channel_id=1, source_target_pairs={{0,14},{2,0},{4,2},{6,4},{8,6},{10,8},{12,10},{14,12},{1,15},{3,1}... | collective-permute-start | bytes 884744 | tf_op jit(solution)/shard_map/combined/ppermute | solution.py:26
  138.0 11.3 %collective-permute-start.29 = (bf16[4,24,1792]{2,1,0:T(8,128)(2,1)S(1)}, bf16[4,24,1792]{2,1,0:T(8,128)(2,1)S(1)}, u32[]{:S(2)}, u32[]{:S(2)}) collective-permute-start(bf16[4,24,1792]{2,1,0:T(8,128)(2,1)S(1)} %get-tuple-element.68), channel_id=1, source_target_pairs={{0,33},{1,32},{32,1},{33,0},{2,35},{3,34},{34,3},{35,2},{4,37},{5,... | collective-permute-start | bytes 1032200 | tf_op jit(solution)/shard_map/gamma/ppermute | solution.py:21
  139.5 10.0 %collective-permute-start.30 = (bf16[4,24,1792]{2,1,0:T(8,128)(2,1)S(1)}, bf16[4,24,1792]{2,1,0:T(8,128)(2,1)S(1)}, u32[]{:S(2)}, u32[]{:S(2)}) collective-permute-start(bf16[4,24,1792]{2,1,0:T(8,128)(2,1)S(1)} %get-tuple-element.69), channel_id=1, source_target_pairs={{0,1},{1,0},{32,33},{33,32},{2,3},{3,2},{34,35},{35,34},{4,5},{5,4... | collective-permute-start | bytes 1032200 | tf_op jit(solution)/shard_map/gamma/ppermute | solution.py:21
  141.1 27.9 %collective-permute-start.32 = (bf16[4,24,1792]{2,1,0:T(8,128)(2,1)S(1)}, bf16[4,24,1792]{2,1,0:T(8,128)(2,1)S(1)}, u32[]{:S(2)}, u32[]{:S(2)}) collective-permute-start(bf16[4,24,1792]{2,1,0:T(8,128)(2,1)S(1)} %get-tuple-element.72), channel_id=1, source_target_pairs={{0,33},{1,32},{32,1},{33,0},{2,35},{3,34},{34,3},{35,2},{4,37},{5,... | collective-permute-start | bytes 1032200 | tf_op jit(solution)/shard_map/gamma/ppermute | solution.py:21
  152.3 20.4 %collective-permute-start.31 = (bf16[4,24,1792]{2,1,0:T(8,128)(2,1)S(1)}, bf16[4,24,1792]{2,1,0:T(8,128)(2,1)S(1)}, u32[]{:S(2)}, u32[]{:S(2)}) collective-permute-start(bf16[4,24,1792]{2,1,0:T(8,128)(2,1)S(1)} %add_convert_fusion.3), channel_id=1, source_target_pairs={{0,1},{1,0},{32,33},{33,32},{2,3},{3,2},{34,35},{35,34},{4,5},{5,4... | collective-permute-start | bytes 1032200 | tf_op jit(solution)/shard_map/gamma/ppermute | solution.py:21
  159.2 13.7 %collective-permute-start.38 = (bf16[24,1792]{1,0:T(8,128)(2,1)S(1)}, bf16[24,1792]{1,0:T(8,128)(2,1)S(1)}, u32[]{:S(2)}, u32[]{:S(2)}) collective-permute-start(bf16[24,1792]{1,0:T(8,128)(2,1)S(1)} %get-tuple-element.80), channel_id=1, source_target_pairs={{0,8},{2,10},{4,12},{6,14},{8,0},{10,2},{12,4},{14,6},{1,9},{3,11}... | collective-permute-start | bytes 258056 | tf_op jit(solution)/shard_map/spread/ppermute | solution.py:26
  162.3 12.7 %collective-permute-start.39 = (bf16[24,1792]{1,0:T(8,128)(2,1)S(1)}, bf16[24,1792]{1,0:T(8,128)(2,1)S(1)}, u32[]{:S(2)}, u32[]{:S(2)}) collective-permute-start(bf16[24,1792]{1,0:T(8,128)(2,1)S(1)} %get-tuple-element.79), channel_id=1, source_target_pairs={{0,10},{2,12},{4,14},{6,0},{8,2},{10,4},{12,6},{14,8},{1,11},{3,13... | collective-permute-start | bytes 258056 | tf_op jit(solution)/shard_map/spread/ppermute | solution.py:26
  165.6 11.0 %collective-permute-start.40 = (bf16[24,1792]{1,0:T(8,128)(2,1)S(1)}, bf16[24,1792]{1,0:T(8,128)(2,1)S(1)}, u32[]{:S(2)}, u32[]{:S(2)}) collective-permute-start(bf16[24,1792]{1,0:T(8,128)(2,1)S(1)} %get-tuple-element.78), channel_id=1, source_target_pairs={{0,12},{2,14},{4,0},{6,2},{8,4},{10,6},{12,8},{14,10},{1,13},{3,15... | collective-permute-start | bytes 258056 | tf_op jit(solution)/shard_map/spread/ppermute | solution.py:26
  174.9 9.6 %collective-permute-start.35 = (bf16[24,1792]{1,0:T(8,128)(2,1)S(1)}, bf16[24,1792]{1,0:T(8,128)(2,1)S(1)}, u32[]{:S(2)}, u32[]{:S(2)}) collective-permute-start(bf16[24,1792]{1,0:T(8,128)(2,1)S(1)} %get-tuple-element.81), channel_id=1, source_target_pairs={{0,6},{2,8},{4,10},{6,12},{8,14},{10,0},{12,2},{14,4},{1,7},{3,9},... | collective-permute-start | bytes 258056 | tf_op jit(solution)/shard_map/spread/ppermute | solution.py:26
  (22 other events, 197.0 us)

commit v2 on v1

--- a/solution.py
+++ b/solution.py
@@ -53,68 +53,69 @@
             at += piece.shape[0]
 
 
-def early_kernel(own, xlf, *refs):
-    near, far, (out, stack, left) = refs[0:3], refs[3:6], refs[6:9]
+def turned(target, row0, piece):
+    def body(n, carry):
+        tile = piece[:, pl.ds(pl.multiple_of(n * BLK, BLK), BLK)]
+        target[pl.ds(pl.multiple_of(row0 + n * BLK, BLK), BLK), :] = tile.T
+        return carry
+
+    lax.fori_loop(0, piece.shape[1] // BLK, body, 0)
+
+
+def early_kernel(own, xlf, bof, *refs):
+    near, far, (out, stack, left, bof_turned) = refs[0:3], refs[3:6], refs[6:10]
     xl, c = lax.axis_index("xl"), lax.axis_index("core")
     rows, half = own.shape
     stacked(stack, near, far)
+    turned(bof_turned, 0, bof)
 
     @pl.when(xl == c)
     def _():
-        lay(left, 0, 0, own)
-        lay(left, 0, half, far[0])
+        turned(left, 0, own)
+        turned(left, half, far[0])
 
     @pl.when(xl != c)
     def _():
-        lay(left, 0, half, own)
-        lay(left, 0, 0, xlf)
+        turned(left, half, own)
+        turned(left, 0, xlf)
 
     def block(n, carry):
-        out[n] = dot_t(left[...], stack[pl.ds(pl.multiple_of(n * rows, 128), rows), :])
+        columns = stack[pl.ds(pl.multiple_of(n * rows, 128), rows), :]
+        out[n] = jnp.dot(columns, left[...], preferred_element_type=F32)
         return carry
 
     lax.fori_loop(0, NY - 1, block, 0)
 
 
-def coulomb_kernel(early, left, bof, xh, many, *refs):
+def coulomb_kernel(early, left, bof_turned, xh, many, *refs):
     near, far, (p0, p1, p2, p3, p5, p6, p7), refs = refs[0:2], refs[2:4], refs[4:11], refs[11:]
     send_up, send_down, keep_up, keep_down, last, out, flipped = refs
     z, xl, c = lax.axis_index("z"), lax.axis_index("xl"), lax.axis_index("core")
-    rows, half = bof.shape
+    rows, half = xh.shape
     stacked(last, near, far)
 
     @pl.when(xl == c)
     def _():
-        lay(flipped, 0, 0, xh)
-        lay(flipped, 0, half, bof)
+        turned(flipped, 0, xh)
+        lay(flipped, half, 0, bof_turned)
 
     @pl.when(xl != c)
     def _():
-        lay(flipped, 0, half, xh)
-        lay(flipped, 0, 0, bof)
+        turned(flipped, half, xh)
+        lay(flipped, 0, 0, bof_turned)
 
     def place(e, d):
         return lax.rem(e * NY + d + NZ - z, NZ)
 
     def block(n, carry):
-        out[place(1, n)] = dot_t(flipped[...], many[pl.ds(pl.multiple_of(n * rows, 128), rows), :])
+        columns = many[pl.ds(pl.multiple_of(n * rows, 128), rows), :]
+        out[place(1, n)] = jnp.dot(columns, flipped[...], preferred_element_type=F32)
         out[place(0, n)] = early[n]
         return carry
 
     lax.fori_loop(0, NY - 1, block, 0)
-
-    def end(e, carry):
-        @pl.when(e == 0)
-        def _():
-            out[place(0, NY - 1)] = dot_t(left[...], last[...])
-
-        @pl.when(e == 1)
-        def _():
-            out[place(1, NY - 1)] = dot_t(flipped[...], last[...])
-
-        return carry
-
-    lax.fori_loop(0, 2, end, 0)
+    out[place(0, NY - 1)] = jnp.dot(last[...], left[...], preferred_element_type=F32)
+    out[place(1, NY - 1)] = jnp.dot(last[...], flipped[...], preferred_element_type=F32)
     low, high = slice(0, rows // 2), slice(rows // 2, rows)
     for k, ref in ((0, p0), (1, p1), (2, p2), (6, p6), (7, p7)):
         ref[...] = out[k]
@@ -133,11 +134,11 @@
     col_occ = ((lax.rem(y + NY - back, NY) * NXH + xh) * NC + xl) * count
     for i in range(count):
         for j in range(count):
-            tile = (pl.ds(i * virt, virt), pl.ds(j * virt, virt))
+            tile = (pl.ds(j * virt, virt), pl.ds(i * virt, virt))
             total = mine[tile] + up[tile].astype(F32) + down[tile].astype(F32)
-            row, col = v_col[...] - occ_ref[row_occ + i], v_row[...] - occ_ref[col_occ + j]
+            row, col = v_row[...] - occ_ref[row_occ + i], v_col[...] - occ_ref[col_occ + j]
             amp = (total / (row + col)).astype(BF).astype(F32)
-            comb = 2.0 * amp - amp.T
+            comb = 2.0 * amp.T - amp
             for zp in range(NZ):
                 for h in range(NXL):
                     at = (zp * NXL + h) * 8
@@ -219,17 +220,18 @@
     with jax.named_scope("coulomb"):
         whole, part = jax.ShapeDtypeStruct((rows, rows), F32), jax.ShapeDtypeStruct((hr, rows), F32)
         sent = jax.ShapeDtypeStruct((hr, rows), BF)
-        early, many, left = pl.pallas_call(
+        early, many, left, bof_turned = pl.pallas_call(
             early_kernel,
             out_shape=[
                 jax.ShapeDtypeStruct((NY - 1, rows, rows), F32),
                 jax.ShapeDtypeStruct(((NY - 1) * rows, 2 * aux), BF),
-                jax.ShapeDtypeStruct((rows, 2 * aux), BF),
+                jax.ShapeDtypeStruct((2 * aux, rows), BF),
+                jax.ShapeDtypeStruct((aux, rows), BF),
             ],
-            in_specs=[vmem] * 8,
-            out_specs=[vmem] * 3,
+            in_specs=[vmem] * 9,
+            out_specs=[vmem] * 4,
             compiler_params=params,
-        )(own, xlf, j0, j1, j3, f0, f1, f3)
+        )(own, xlf, bof, j0, j1, j3, f0, f1, f3)
         early, j2a, j2b, xh = lax.optimization_barrier((early, j2a, j2b, xh))
         f2a, f2b = flip_core(j2a), flip_core(j2b)
         mine, p1, p2, p3, p5, p6, p7, up, down, keep_up, keep_down, last = pl.pallas_call(
@@ -238,9 +240,9 @@
             + [jax.ShapeDtypeStruct((rows, 2 * aux), BF)],
             in_specs=[vmem] * 9,
             out_specs=[vmem] * 12,
-            scratch_shapes=[pltpu.VMEM((NZ, rows, rows), F32), pltpu.VMEM((rows, 2 * aux), BF)],
+            scratch_shapes=[pltpu.VMEM((NZ, rows, rows), F32), pltpu.VMEM((2 * aux, rows), BF)],
             compiler_params=params,
-        )(early, left, bof, xh, many, j2a, j2b, f2a, f2b)
+        )(early, left, bof_turned, xh, many, j2a, j2b, f2a, f2b)
 
     with jax.named_scope("ring"):
         up, down = shift(up, "z", 1), shift(down, "z", -1)

time: 186 us -> 185 us (level)
  waiting for transfers between devices: 71.3 us -> 66.5 us
  Pallas kernels: 28.8 us -> 31 us
    ppermute x27, waiting for transfers between devices: 54.3 us -> 50.7 us  [shift(): lax.ppermute(value, axis, [(i, (i + steps) % count) for i in range(count)])]
    pallas_call x1, Pallas kernels: 5.29 us -> 8.04 us  [on_device(): pl.pallas_call(early_kernel, out_shape=[jax.ShapeDtypeStruct((NY - 1, row...]
  transfers between devices with their start and end apart: 42 -> 42, of which waited for: 25 -> 22; matrix products, arithmetic and copies ran while one was open for 1% -> 1% of each run, Pallas kernels for 6% -> 8%
where the time goes in v2:
time: 185 us
  starting transfers between devices  83.5 us (45%)
  waiting for transfers between devices  66.5 us (36%)
  Pallas kernels  31 us (17%)
  other arithmetic  2.53 us (1%)
    ppermute x27, starting transfers between devices, shift(): lax.ppermute(value, axis, [(i, (i + steps) % count) for i in range(count)])  51.7 us
    ppermute x27, waiting for transfers between devices, shift(): lax.ppermute(value, axis, [(i, (i + steps) % count) for i in range(count)])  50.7 us
    ppermute x8, starting transfers between devices, flip_x(): return lax.ppermute(value, X, [(i, i ^ bits) for i in range(NXH * NXL)])  15.5 us
    pallas_call x2, Pallas kernels, gamma_of(): pl.pallas_call(functools.partial(gamma_kernel, group=group), out_shape=[j...  12.1 us
    ppermute x8, waiting for transfers between devices, flip_x(): return lax.ppermute(value, X, [(i, i ^ bits) for i in range(NXH * NXL)])  11.6 us
    ppermute x1, starting transfers between devices, on_device(): xlf = lax.ppermute(own, ('core', 'xl'), [(0, 1), (3, 2)])  10.6 us
    pallas_call x1, Pallas kernels, on_device(): pl.pallas_call(coulomb_kernel, out_shape=[whole, whole, whole, part, part...  8.91 us
    pallas_call x1, Pallas kernels, on_device(): pl.pallas_call(early_kernel, out_shape=[jax.ShapeDtypeStruct((NY - 1, row...  8.04 us
  transfers between devices with their start and end apart: 42, of which 22 were waited for; matrix products, arithmetic and copies ran while one was open for 1% of the time, Pallas kernels for 8%

profile of v2, /device:TPU:32, one launch (start us, length us, event | category | flops | bytes accessed | tf_op | source)
XLA Modules:
  0.0 185.0 jit_solution(18153265084829566914)
XLA Ops:
  2.7 4.3 %collective-permute-start.5 = (bf16[384,896]{1,0:T(8,128)(2,1)S(1)}, bf16[384,896]{1,0:T(8,128)(2,1)S(1)}, u32[]{:S(2)}, u32[]{:S(2)}) collective-permute-start(bf16[384,896]{1,0:T(8,128)(2,1)S(1)} %bitcast.29), channel_id=1, source_target_pairs={{0,33},{1,32},{32,1},{33,0},{2,35},{3,34},{34,3},{35,2},{4,37},{5,... | collective-permute-start | bytes 2064392 | tf_op jit(solution)/shard_map/gather/ppermute | solution.py:21
  10.2 10.6 %collective-permute-start.2 = (bf16[384,896]{1,0:T(8,128)(2,1)S(1)}, bf16[384,896]{1,0:T(8,128)(2,1)S(1)}, u32[]{:S(2)}, u32[]{:S(2)}) collective-permute-start(bf16[384,896]{1,0:T(8,128)(2,1)S(1)} %bitcast.30), channel_id=1, source_target_pairs={{0,1},{17,16},{2,3},{19,18},{4,5},{21,20},{6,7},{23,22},{8,9},{25,... | collective-permute-start | bytes 2064392 | tf_op jit(solution)/shard_map/gather/ppermute | solution.py:207
  22.5 4.2 %collective-permute-start.6 = (bf16[384,896]{1,0:T(8,128)(2,1)S(1)}, bf16[384,896]{1,0:T(8,128)(2,1)S(1)}, u32[]{:S(2)}, u32[]{:S(2)}) collective-permute-start(bf16[384,896]{1,0:T(8,128)(2,1)S(1)} %collective-permute-done.3.refs_1_), channel_id=1, source_target_pairs={{0,16},{16,0},{1,17},{17,1},{2,18},{18,2},{3,19},{19,3},{4,20},{20... | collective-permute-start | bytes 2064392 | tf_op jit(solution)/shard_map/gather/ppermute | solution.py:30
  36.2 8.0 %coulomb.2 = (f32[3,384,384]{2,1,0:T(8,128)}, bf16[1152,1792]{1,0:T(8,128)(2,1)}, bf16[1792,384]{1,0:T(8,128)(2,1)}, bf16[896,384]{1,0:T(8,128)(2,1)S(1)}) custom-call(bf16[384,896]{1,0:T(8,128)(2,1)S(1)} %bitcast.32, bf16[384,896]{1,0:T(8,128)(2,1)S(1)} %collective-permute-done.2.xlf, bf16[384,896]{1,0:T(8,128)(2,1)S(1)} %collective-permute-done.5.bof, ...), custom_call_target="tpu_custom_call" | custom-call | tf_op jit(solution)/shard_map/coulomb/pallas_call | solution.py:223
  49.8 8.9 %coulomb.3 = (f32[384,384]{1,0:T(8,128)S(1)}, f32[384,384]{1,0:T(8,128)S(1)}, f32[384,384]{1,0:T(8,128)S(1)}, f32[192,384]{1,0:T(8,128)S(1)}, f32[192,384]{1,0:T...) custom-call(f32[3,384,384]{2,1,0:T(8,128)} %get-tuple-element.49.ear, ...), custom_call_target="tpu_custom_call" | custom-call | tf_op jit(solution)/shard_map/coulomb/pallas_call | solution.py:237
  60.8 4.0 %collective-permute-done.17 = bf16[192,384]{1,0:T(8,128)(2,1)S(1)} collective-permute-done((bf16[192,384]{1,0:T(8,128)(2,1)S(1)}, bf16[192,384]{1,0:T(8,128)(2,1)S(1)}, u32[]{:S(2)}, u32[]{:S(2)}) %collective-permute-start.17) | collective-permute-done | bytes 147488 | tf_op jit(solution)/shard_map/ring/ppermute | solution.py:26
  64.9 3.6 %collective-permute-start.18 = (bf16[384,384]{1,0:T(8,128)(2,1)S(1)}, bf16[384,384]{1,0:T(8,128)(2,1)S(1)}, u32[]{:S(2)}, u32[]{:S(2)}) collective-permute-start(bf16[384,384]{1,0:T(8,128)(2,1)S(1)} %pad_maximum_fusion.1), channel_id=1, source_target_pairs={{0,14},{2,0},{4,2},{6,4},{8,6},{10,8},{12,10},{14,12},{1,15},{3,1}... | collective-permute-start | bytes 884744 | tf_op jit(solution)/shard_map/ring/ppermute | solution.py:26
  68.8 5.5 %collective-permute-done.18 = bf16[384,384]{1,0:T(8,128)(2,1)S(1)} collective-permute-done((bf16[384,384]{1,0:T(8,128)(2,1)S(1)}, bf16[384,384]{1,0:T(8,128)(2,1)S(1)}, u32[]{:S(2)}, u32[]{:S(2)}) %collective-permute-start.18) | collective-permute-done | bytes 294944 | tf_op jit(solution)/shard_map/ring/ppermute | solution.py:26
  74.3 3.8 %collective-permute-start.19 = (bf16[384,384]{1,0:T(8,128)(2,1)S(1)}, bf16[384,384]{1,0:T(8,128)(2,1)S(1)}, u32[]{:S(2)}, u32[]{:S(2)}) collective-permute-start(bf16[384,384]{1,0:T(8,128)(2,1)S(1)} %add_convert_fusion.5), channel_id=1, source_target_pairs={{0,14},{2,0},{4,2},{6,4},{8,6},{10,8},{12,10},{14,12},{1,15},{3,1}... | collective-permute-start | bytes 884744 | tf_op jit(solution)/shard_map/ring/ppermute | solution.py:26
  78.7 4.4 %collective-permute-done.19 = bf16[384,384]{1,0:T(8,128)(2,1)S(1)} collective-permute-done((bf16[384,384]{1,0:T(8,128)(2,1)S(1)}, bf16[384,384]{1,0:T(8,128)(2,1)S(1)}, u32[]{:S(2)}, u32[]{:S(2)}) %collective-permute-start.19) | collective-permute-done | bytes 294944 | tf_op jit(solution)/shard_map/ring/ppermute | solution.py:26
  83.2 3.5 %collective-permute-start.20 = (bf16[384,384]{1,0:T(8,128)(2,1)S(1)}, bf16[384,384]{1,0:T(8,128)(2,1)S(1)}, u32[]{:S(2)}, u32[]{:S(2)}) collective-permute-start(bf16[384,384]{1,0:T(8,128)(2,1)S(1)} %add_convert_fusion.4), channel_id=1, source_target_pairs={{0,14},{2,0},{4,2},{6,4},{8,6},{10,8},{12,10},{14,12},{1,15},{3,1}... | collective-permute-start | bytes 884744 | tf_op jit(solution)/shard_map/ring/ppermute | solution.py:26
  87.4 3.6 %collective-permute-done.20.down = bf16[384,384]{1,0:T(8,128)(2,1)S(1)} collective-permute-done((bf16[384,384]{1,0:T(8,128)(2,1)S(1)}, bf16[384,384]{1,0:T(8,128)(2,1)S(1)}, u32[]{:S(2)}, u32[]{:S(2)}) %collective-permute-start.20) | collective-permute-done | bytes 294944 | tf_op jit(solution)/shard_map/ring/ppermute | solution.py:26
  91.0 4.2 %collective-permute-done.16.up = bf16[384,384]{1,0:T(8,128)(2,1)S(1)} collective-permute-done((bf16[384,384]{1,0:T(8,128)(2,1)S(1)}, bf16[384,384]{1,0:T(8,128)(2,1)S(1)}, u32[]{:S(2)}, u32[]{:S(2)}) %collective-permute-start.16) | collective-permute-done | bytes 294944 | tf_op jit(solution)/shard_map/ring/ppermute | solution.py:26
  99.7 5.6 %collective-permute-done.21.refs_1_ = bf16[2,192,384]{2,1,0:T(8,128)(2,1)S(1)} collective-permute-done((bf16[2,192,384]{2,1,0:T(8,128)(2,1)S(1)}, bf16[2,192,384]{2,1,0:T(8,128)(2,1)S(1)}, u32[]{:S(2)}, u32[]{:S(2)}) %collective-permute-start.21) | collective-permute-done | bytes 294944 | tf_op jit(solution)/shard_map/combined/ppermute | solution.py:26
  105.3 3.5 %collective-permute-start.24 = (bf16[2,192,384]{2,1,0:T(8,128)(2,1)S(1)}, bf16[2,192,384]{2,1,0:T(8,128)(2,1)S(1)}, u32[]{:S(2)}, u32[]{:S(2)}) collective-permute-start(bf16[2,192,384]{2,1,0:T(8,128)(2,1)S(1)} %collective-permute-done.22.refs_2_), channel_id=1, source_target_pairs={{0,14},{2,0},{4,2},{6,4},{8,6},{10,8},{12,10},{14,12},{1,15},{3,1}... | collective-permute-start | bytes 884744 | tf_op jit(solution)/shard_map/combined/ppermute | solution.py:26
  108.8 6.8 %collective-permute-done.23.refs_3_ = bf16[2,192,384]{2,1,0:T(8,128)(2,1)S(1)} collective-permute-done((bf16[2,192,384]{2,1,0:T(8,128)(2,1)S(1)}, bf16[2,192,384]{2,1,0:T(8,128)(2,1)S(1)}, u32[]{:S(2)}, u32[]{:S(2)}) %collective-permute-start.23) | collective-permute-done | bytes 294944 | tf_op jit(solution)/shard_map/combined/ppermute | solution.py:26
  115.6 3.7 %collective-permute-start.26 = (bf16[2,192,384]{2,1,0:T(8,128)(2,1)S(1)}, bf16[2,192,384]{2,1,0:T(8,128)(2,1)S(1)}, u32[]{:S(2)}, u32[]{:S(2)}) collective-permute-start(bf16[2,192,384]{2,1,0:T(8,128)(2,1)S(1)} %collective-permute-done.24.refs_4_), channel_id=1, source_target_pairs={{0,14},{2,0},{4,2},{6,4},{8,6},{10,8},{12,10},{14,12},{1,15},{3,1}... | collective-permute-start | bytes 884744 | tf_op jit(solution)/shard_map/combined/ppermute | solution.py:26
  119.3 6.1 %collective-permute-done.25.refs_5_ = bf16[2,192,384]{2,1,0:T(8,128)(2,1)S(1)} collective-permute-done((bf16[2,192,384]{2,1,0:T(8,128)(2,1)S(1)}, bf16[2,192,384]{2,1,0:T(8,128)(2,1)S(1)}, u32[]{:S(2)}, u32[]{:S(2)}) %collective-permute-start.25) | collective-permute-done | bytes 294944 | tf_op jit(solution)/shard_map/combined/ppermute | solution.py:26
  131.6 6.0 %gamma.3 = (bf16[4,24,1792]{2,1,0:T(8,128)(2,1)S(1)}, bf16[4,24,1792]{2,1,0:T(8,128)(2,1)S(1)}, bf16[4,24,1792]{2,1,0:T(8,128)(2,1)S(1)}, f32[4,24,1792]{2,1,0:T(8,128)S(1)}) custom-call(bf16[2,192,384]{2,1,0:T(8,128)(2,1)S(1)} %combined.1.refs_0_, bf16[2,192,384]{2,1,0:T(8,128)(2,1)S(1)} %collective-permute-done.21.refs_1_, ...), custom_call_target="tpu_custom_call" | custom-call | tf_op jit(solution)/shard_map/gamma/pallas_call | solution.py:276
  141.5 6.1 %gamma.2 = (f32[4,24,1792]{2,1,0:T(8,128)S(1)}, f32[4,24,1792]{2,1,0:T(8,128)S(1)}, f32[4,24,1792]{2,1,0:T(8,128)S(1)}, bf16[4,24,1792]{2,1,0:T(8,128)(2,1)S(1)}) custom-call(bf16[2,192,384]{2,1,0:T(8,128)(2,1)S(1)} %combined.1.refs_0_, bf16[2,192,384]{2,1,0:T(8,128)(2,1)S(1)} %collective-permute-done.21.refs_1_, ...), custom_call_target="tpu_custom_call" | custom-call | tf_op jit(solution)/shard_map/gamma/pallas_call | solution.py:276
  154.0 3.9 %collective-permute-done.37 = bf16[4,24,1792]{2,1,0:T(8,128)(2,1)S(1)} collective-permute-done((bf16[4,24,1792]{2,1,0:T(8,128)(2,1)S(1)}, bf16[4,24,1792]{2,1,0:T(8,128)(2,1)S(1)}, u32[]{:S(2)}, u32[]{:S(2)}) %collective-permute-start.37) | collective-permute-done | bytes 344096 | tf_op jit(solution)/shard_map/gamma/ppermute | solution.py:21
  162.3 3.4 %collective-permute-start.39 = (bf16[24,1792]{1,0:T(8,128)(2,1)S(1)}, bf16[24,1792]{1,0:T(8,128)(2,1)S(1)}, u32[]{:S(2)}, u32[]{:S(2)}) collective-permute-start(bf16[24,1792]{1,0:T(8,128)(2,1)S(1)} %get-tuple-element.81), channel_id=1, source_target_pairs={{0,10},{2,12},{4,14},{6,0},{8,2},{10,4},{12,6},{14,8},{1,11},{3,13... | collective-permute-start | bytes 258056 | tf_op jit(solution)/shard_map/spread/ppermute | solution.py:26
  168.9 3.4 %collective-permute-start.41 = (bf16[24,1792]{1,0:T(8,128)(2,1)S(1)}, bf16[24,1792]{1,0:T(8,128)(2,1)S(1)}, u32[]{:S(2)}, u32[]{:S(2)}) collective-permute-start(bf16[24,1792]{1,0:T(8,128)(2,1)S(1)} %get-tuple-element.79), channel_id=1, source_target_pairs={{0,14},{2,0},{4,2},{6,4},{8,6},{10,8},{12,10},{14,12},{1,15},{3,1}... | collective-permute-start | bytes 258056 | tf_op jit(solution)/shard_map/spread/ppermute | solution.py:26
  179.2 4.8 %collective-permute-done.35.refs_3_ = bf16[24,1792]{1,0:T(8,128)(2,1)S(1)} collective-permute-done((bf16[24,1792]{1,0:T(8,128)(2,1)S(1)}, bf16[24,1792]{1,0:T(8,128)(2,1)S(1)}, u32[]{:S(2)}, u32[]{:S(2)}) %collective-permute-start.35) | collective-permute-done | bytes 86048 | tf_op jit(solution)/shard_map/spread/ppermute | solution.py:26
  (100 shorter events, 62.6 us)
Async XLA Ops:
  2.7 19.8 %collective-permute-start.5 = (bf16[384,896]{1,0:T(8,128)(2,1)S(1)}, bf16[384,896]{1,0:T(8,128)(2,1)S(1)}, u32[]{:S(2)}, u32[]{:S(2)}) collective-permute-start(bf16[384,896]{1,0:T(8,128)(2,1)S(1)} %bitcast.29), channel_id=1, source_target_pairs={{0,33},{1,32},{32,1},{33,0},{2,35},{3,34},{34,3},{35,2},{4,37},{5,... | collective-permute-start | bytes 2064392 | tf_op jit(solution)/shard_map/gather/ppermute | solution.py:21
  7.0 15.5 %collective-permute-start.3 = (bf16[384,896]{1,0:T(8,128)(2,1)S(1)}, bf16[384,896]{1,0:T(8,128)(2,1)S(1)}, u32[]{:S(2)}, u32[]{:S(2)}) collective-permute-start(bf16[384,896]{1,0:T(8,128)(2,1)S(1)} %collective-permute-done.refs_0_), channel_id=1, source_target_pairs={{0,64},{64,128},{128,192},{192,0},{1,65},{65,129},{129,193},{193,1... | collective-permute-start | bytes 2064392 | tf_op jit(solution)/shard_map/gather/ppermute | solution.py:26
  8.6 13.9 %collective-permute-start.4 = (bf16[384,896]{1,0:T(8,128)(2,1)S(1)}, bf16[384,896]{1,0:T(8,128)(2,1)S(1)}, u32[]{:S(2)}, u32[]{:S(2)}) collective-permute-start(bf16[384,896]{1,0:T(8,128)(2,1)S(1)} %collective-permute-done.refs_0_), channel_id=1, source_target_pairs={{0,192},{64,0},{128,64},{192,128},{1,193},{65,1},{129,65},{193,129... | collective-permute-start | bytes 2064392 | tf_op jit(solution)/shard_map/gather/ppermute | solution.py:26
  10.2 19.1 %collective-permute-start.2 = (bf16[384,896]{1,0:T(8,128)(2,1)S(1)}, bf16[384,896]{1,0:T(8,128)(2,1)S(1)}, u32[]{:S(2)}, u32[]{:S(2)}) collective-permute-start(bf16[384,896]{1,0:T(8,128)(2,1)S(1)} %bitcast.30), channel_id=1, source_target_pairs={{0,1},{17,16},{2,3},{19,18},{4,5},{21,20},{6,7},{23,22},{8,9},{25,... | collective-permute-start | bytes 2064392 | tf_op jit(solution)/shard_map/gather/ppermute | solution.py:207
  22.5 12.9 %collective-permute-start.6 = (bf16[384,896]{1,0:T(8,128)(2,1)S(1)}, bf16[384,896]{1,0:T(8,128)(2,1)S(1)}, u32[]{:S(2)}, u32[]{:S(2)}) collective-permute-start(bf16[384,896]{1,0:T(8,128)(2,1)S(1)} %collective-permute-done.3.refs_1_), channel_id=1, source_target_pairs={{0,16},{16,0},{1,17},{17,1},{2,18},{18,2},{3,19},{19,3},{4,20},{20... | collective-permute-start | bytes 2064392 | tf_op jit(solution)/shard_map/gather/ppermute | solution.py:30
  29.3 18.4 %collective-permute-start.10 = (bf16[384,896]{1,0:T(8,128)(2,1)S(1)}, bf16[384,896]{1,0:T(8,128)(2,1)S(1)}, u32[]{:S(2)}, u32[]{:S(2)}) collective-permute-start(bf16[384,896]{1,0:T(8,128)(2,1)S(1)} %bitcast.31), channel_id=1, source_target_pairs={{0,32},{1,33},{32,0},{33,1},{2,34},{3,35},{34,2},{35,3},{4,36},{5,... | collective-permute-start | bytes 2064392 | tf_op jit(solution)/shard_map/gather/ppermute | solution.py:21
  32.1 12.2 %collective-permute-start.8 = (bf16[192,896]{1,0:T(8,128)(2,1)S(1)}, bf16[192,896]{1,0:T(8,128)(2,1)S(1)}, u32[]{:S(2)}, u32[]{:S(2)}) collective-permute-start(bf16[192,896]{1,0:T(8,128)(2,1)S(1)} %slice.36), channel_id=1, source_target_pairs={{0,64},{64,128},{128,192},{192,0},{1,65},{65,129},{129,193},{193,1... | collective-permute-start | bytes 1032200 | tf_op jit(solution)/shard_map/gather/ppermute | solution.py:26
  32.5 11.8 %collective-permute-start.9 = (bf16[192,896]{1,0:T(8,128)(2,1)S(1)}, bf16[192,896]{1,0:T(8,128)(2,1)S(1)}, u32[]{:S(2)}, u32[]{:S(2)}) collective-permute-start(bf16[192,896]{1,0:T(8,128)(2,1)S(1)} %slice.37), channel_id=1, source_target_pairs={{0,192},{64,0},{128,64},{192,128},{1,193},{65,1},{129,65},{193,129... | collective-permute-start | bytes 1032200 | tf_op jit(solution)/shard_map/gather/ppermute | solution.py:26
  58.9 9.7 %collective-permute-start.13 = (bf16[192,384]{1,0:T(8,128)(2,1)S(1)}, bf16[192,384]{1,0:T(8,128)(2,1)S(1)}, u32[]{:S(2)}, u32[]{:S(2)}) collective-permute-start(bf16[192,384]{1,0:T(8,128)(2,1)S(1)} %get-tuple-element.57), channel_id=1, source_target_pairs={{0,2},{2,4},{4,6},{6,8},{8,10},{10,12},{12,14},{14,0},{1,3},{3,5},... | collective-permute-start | bytes 442376 | tf_op jit(solution)/shard_map/ring/ppermute | solution.py:26
  64.9 9.3 %collective-permute-start.18 = (bf16[384,384]{1,0:T(8,128)(2,1)S(1)}, bf16[384,384]{1,0:T(8,128)(2,1)S(1)}, u32[]{:S(2)}, u32[]{:S(2)}) collective-permute-start(bf16[384,384]{1,0:T(8,128)(2,1)S(1)} %pad_maximum_fusion.1), channel_id=1, source_target_pairs={{0,14},{2,0},{4,2},{6,4},{8,6},{10,8},{12,10},{14,12},{1,15},{3,1}... | collective-permute-start | bytes 884744 | tf_op jit(solution)/shard_map/ring/ppermute | solution.py:26
  68.7 9.8 %collective-permute-start.14 = (bf16[384,384]{1,0:T(8,128)(2,1)S(1)}, bf16[384,384]{1,0:T(8,128)(2,1)S(1)}, u32[]{:S(2)}, u32[]{:S(2)}) collective-permute-start(bf16[384,384]{1,0:T(8,128)(2,1)S(1)} %pad_maximum_fusion), channel_id=1, source_target_pairs={{0,2},{2,4},{4,6},{6,8},{8,10},{10,12},{12,14},{14,0},{1,3},{3,5},... | collective-permute-start | bytes 884744 | tf_op jit(solution)/shard_map/ring/ppermute | solution.py:26
  96.3 9.0 %collective-permute-start.21 = (bf16[2,192,384]{2,1,0:T(8,128)(2,1)S(1)}, bf16[2,192,384]{2,1,0:T(8,128)(2,1)S(1)}, u32[]{:S(2)}, u32[]{:S(2)}) collective-permute-start(bf16[2,192,384]{2,1,0:T(8,128)(2,1)S(1)} %combined.1.refs_0_), channel_id=1, source_target_pairs={{0,2},{2,4},{4,6},{6,8},{8,10},{10,12},{12,14},{14,0},{1,3},{3,5},... | collective-permute-start | bytes 884744 | tf_op jit(solution)/shard_map/combined/ppermute | solution.py:26
  105.3 10.3 %collective-permute-start.23 = (bf16[2,192,384]{2,1,0:T(8,128)(2,1)S(1)}, bf16[2,192,384]{2,1,0:T(8,128)(2,1)S(1)}, u32[]{:S(2)}, u32[]{:S(2)}) collective-permute-start(bf16[2,192,384]{2,1,0:T(8,128)(2,1)S(1)} %collective-permute-done.21.refs_1_), channel_id=1, source_target_pairs={{0,2},{2,4},{4,6},{6,8},{8,10},{10,12},{12,14},{14,0},{1,3},{3,5},... | collective-permute-start | bytes 884744 | tf_op jit(solution)/shard_map/combined/ppermute | solution.py:26
  105.3 10.3 %collective-permute-start.24 = (bf16[2,192,384]{2,1,0:T(8,128)(2,1)S(1)}, bf16[2,192,384]{2,1,0:T(8,128)(2,1)S(1)}, u32[]{:S(2)}, u32[]{:S(2)}) collective-permute-start(bf16[2,192,384]{2,1,0:T(8,128)(2,1)S(1)} %collective-permute-done.22.refs_2_), channel_id=1, source_target_pairs={{0,14},{2,0},{4,2},{6,4},{8,6},{10,8},{12,10},{14,12},{1,15},{3,1}... | collective-permute-start | bytes 884744 | tf_op jit(solution)/shard_map/combined/ppermute | solution.py:26
  115.6 9.8 %collective-permute-start.25 = (bf16[2,192,384]{2,1,0:T(8,128)(2,1)S(1)}, bf16[2,192,384]{2,1,0:T(8,128)(2,1)S(1)}, u32[]{:S(2)}, u32[]{:S(2)}) collective-permute-start(bf16[2,192,384]{2,1,0:T(8,128)(2,1)S(1)} %collective-permute-done.23.refs_3_), channel_id=1, source_target_pairs={{0,2},{2,4},{4,6},{6,8},{8,10},{10,12},{12,14},{14,0},{1,3},{3,5},... | collective-permute-start | bytes 884744 | tf_op jit(solution)/shard_map/combined/ppermute | solution.py:26
  115.6 9.9 %collective-permute-start.26 = (bf16[2,192,384]{2,1,0:T(8,128)(2,1)S(1)}, bf16[2,192,384]{2,1,0:T(8,128)(2,1)S(1)}, u32[]{:S(2)}, u32[]{:S(2)}) collective-permute-start(bf16[2,192,384]{2,1,0:T(8,128)(2,1)S(1)} %collective-permute-done.24.refs_4_), channel_id=1, source_target_pairs={{0,14},{2,0},{4,2},{6,4},{8,6},{10,8},{12,10},{14,12},{1,15},{3,1}... | collective-permute-start | bytes 884744 | tf_op jit(solution)/shard_map/combined/ppermute | solution.py:26
  137.6 11.8 %collective-permute-start.29 = (bf16[4,24,1792]{2,1,0:T(8,128)(2,1)S(1)}, bf16[4,24,1792]{2,1,0:T(8,128)(2,1)S(1)}, u32[]{:S(2)}, u32[]{:S(2)}) collective-permute-start(bf16[4,24,1792]{2,1,0:T(8,128)(2,1)S(1)} %get-tuple-element.70), channel_id=1, source_target_pairs={{0,33},{1,32},{32,1},{33,0},{2,35},{3,34},{34,3},{35,2},{4,37},{5,... | collective-permute-start | bytes 1032200 | tf_op jit(solution)/shard_map/gamma/ppermute | solution.py:21
  139.3 10.1 %collective-permute-start.30 = (bf16[4,24,1792]{2,1,0:T(8,128)(2,1)S(1)}, bf16[4,24,1792]{2,1,0:T(8,128)(2,1)S(1)}, u32[]{:S(2)}, u32[]{:S(2)}) collective-permute-start(bf16[4,24,1792]{2,1,0:T(8,128)(2,1)S(1)} %get-tuple-element.71), channel_id=1, source_target_pairs={{0,1},{1,0},{32,33},{33,32},{2,3},{3,2},{34,35},{35,34},{4,5},{5,4... | collective-permute-start | bytes 1032200 | tf_op jit(solution)/shard_map/gamma/ppermute | solution.py:21
  140.8 28.1 %collective-permute-start.32 = (bf16[4,24,1792]{2,1,0:T(8,128)(2,1)S(1)}, bf16[4,24,1792]{2,1,0:T(8,128)(2,1)S(1)}, u32[]{:S(2)}, u32[]{:S(2)}) collective-permute-start(bf16[4,24,1792]{2,1,0:T(8,128)(2,1)S(1)} %get-tuple-element.74), channel_id=1, source_target_pairs={{0,33},{1,32},{32,1},{33,0},{2,35},{3,34},{34,3},{35,2},{4,37},{5,... | collective-permute-start | bytes 1032200 | tf_op jit(solution)/shard_map/gamma/ppermute | solution.py:21
  152.1 20.3 %collective-permute-start.31 = (bf16[4,24,1792]{2,1,0:T(8,128)(2,1)S(1)}, bf16[4,24,1792]{2,1,0:T(8,128)(2,1)S(1)}, u32[]{:S(2)}, u32[]{:S(2)}) collective-permute-start(bf16[4,24,1792]{2,1,0:T(8,128)(2,1)S(1)} %add_convert_fusion.3), channel_id=1, source_target_pairs={{0,1},{1,0},{32,33},{33,32},{2,3},{3,2},{34,35},{35,34},{4,5},{5,4... | collective-permute-start | bytes 1032200 | tf_op jit(solution)/shard_map/gamma/ppermute | solution.py:21
  159.2 13.3 %collective-permute-start.38 = (bf16[24,1792]{1,0:T(8,128)(2,1)S(1)}, bf16[24,1792]{1,0:T(8,128)(2,1)S(1)}, u32[]{:S(2)}, u32[]{:S(2)}) collective-permute-start(bf16[24,1792]{1,0:T(8,128)(2,1)S(1)} %get-tuple-element.82), channel_id=1, source_target_pairs={{0,8},{2,10},{4,12},{6,14},{8,0},{10,2},{12,4},{14,6},{1,9},{3,11}... | collective-permute-start | bytes 258056 | tf_op jit(solution)/shard_map/spread/ppermute | solution.py:26
  162.3 12.6 %collective-permute-start.39 = (bf16[24,1792]{1,0:T(8,128)(2,1)S(1)}, bf16[24,1792]{1,0:T(8,128)(2,1)S(1)}, u32[]{:S(2)}, u32[]{:S(2)}) collective-permute-start(bf16[24,1792]{1,0:T(8,128)(2,1)S(1)} %get-tuple-element.81), channel_id=1, source_target_pairs={{0,10},{2,12},{4,14},{6,0},{8,2},{10,4},{12,6},{14,8},{1,11},{3,13... | collective-permute-start | bytes 258056 | tf_op jit(solution)/shard_map/spread/ppermute | solution.py:26
  165.6 12.1 %collective-permute-start.40 = (bf16[24,1792]{1,0:T(8,128)(2,1)S(1)}, bf16[24,1792]{1,0:T(8,128)(2,1)S(1)}, u32[]{:S(2)}, u32[]{:S(2)}) collective-permute-start(bf16[24,1792]{1,0:T(8,128)(2,1)S(1)} %get-tuple-element.80), channel_id=1, source_target_pairs={{0,12},{2,14},{4,0},{6,2},{8,4},{10,6},{12,8},{14,10},{1,13},{3,15... | collective-permute-start | bytes 258056 | tf_op jit(solution)/shard_map/spread/ppermute | solution.py:26
  174.8 9.3 %collective-permute-start.35 = (bf16[24,1792]{1,0:T(8,128)(2,1)S(1)}, bf16[24,1792]{1,0:T(8,128)(2,1)S(1)}, u32[]{:S(2)}, u32[]{:S(2)}) collective-permute-start(bf16[24,1792]{1,0:T(8,128)(2,1)S(1)} %get-tuple-element.83), channel_id=1, source_target_pairs={{0,6},{2,8},{4,10},{6,12},{8,14},{10,0},{12,2},{14,4},{1,7},{3,9},... | collective-permute-start | bytes 258056 | tf_op jit(solution)/shard_map/spread/ppermute | solution.py:26
  (23 other events, 199.8 us)

commit v3 on v2

--- a/solution.py
+++ b/solution.py
@@ -163,11 +163,11 @@
                 at = fl * half + row0
                 left[at:at + ref.shape[1], cols] = ref[lax.rem(xl + fl, 2)]
 
-    width = 2 * BLK
+    width = many.shape[1] // 2
     piece = half // NZ
 
     def columns(n, carry):
-        cols = pl.ds(pl.multiple_of(n * width, width), width)
+        cols = pl.ds(pl.multiple_of(n * width, BLK), width)
         acc = jnp.dot(left[:, :many.shape[0]], many[:, cols], preferred_element_type=F32)
         acc += jnp.dot(left[:, many.shape[0]:], last[:, cols], preferred_element_type=F32)
         for zp in range(NZ):
@@ -232,8 +232,9 @@
             out_specs=[vmem] * 4,
             compiler_params=params,
         )(own, xlf, bof, j0, j1, j3, f0, f1, f3)
-        early, j2a, j2b, xh = lax.optimization_barrier((early, j2a, j2b, xh))
+        early, j2a, j2b = lax.optimization_barrier((early, j2a, j2b))
         f2a, f2b = flip_core(j2a), flip_core(j2b)
+        f2a, f2b, xh = lax.optimization_barrier((f2a, f2b, xh))
         mine, p1, p2, p3, p5, p6, p7, up, down, keep_up, keep_down, last = pl.pallas_call(
             coulomb_kernel,
             out_shape=[whole, whole, whole, part, part, whole, whole, sent, sent, sent, sent]

time: 185 us -> 186 us (level)
  starting transfers between devices: 83.5 us -> 79.6 us
  waiting for transfers between devices: 66.5 us -> 70.2 us
    ppermute x8, waiting for transfers between devices: 11.6 us -> 17.3 us  [flip_x(): return lax.ppermute(value, X, [(i, i ^ bits) for i in range(NXH * NXL)])]
    ppermute x27, starting transfers between devices: 51.7 us -> 49.1 us  [shift(): lax.ppermute(value, axis, [(i, (i + steps) % count) for i in range(count)])]
  transfers between devices with their start and end apart: 42 -> 42, of which waited for: 22 -> 21; matrix products, arithmetic and copies ran while one was open for 1% -> 1% of each run, Pallas kernels for 8% -> 7%
where the time goes in v3:
time: 186 us; the launch traced here: 185 us
  starting transfers between devices  79.6 us (43%)
  waiting for transfers between devices  70.2 us (38%)
  Pallas kernels  30.6 us (16%)
  other arithmetic  2.53 us (1%)
  local copies, waits for them, and re-layouts  2.04 us (1%)
    ppermute x27, waiting for transfers between devices, shift(): lax.ppermute(value, axis, [(i, (i + steps) % count) for i in range(count)])  52 us
    ppermute x27, starting transfers between devices, shift(): lax.ppermute(value, axis, [(i, (i + steps) % count) for i in range(count)])  49.1 us
    ppermute x8, waiting for transfers between devices, flip_x(): return lax.ppermute(value, X, [(i, i ^ bits) for i in range(NXH * NXL)])  17.3 us
    ppermute x8, starting transfers between devices, flip_x(): return lax.ppermute(value, X, [(i, i ^ bits) for i in range(NXH * NXL)])  14.3 us
    pallas_call x2, Pallas kernels, gamma_of(): pl.pallas_call(functools.partial(gamma_kernel, group=group), out_shape=[j...  11.7 us
    ppermute x1, starting transfers between devices, on_device(): xlf = lax.ppermute(own, ('core', 'xl'), [(0, 1), (3, 2)])  10.6 us
    pallas_call x1, Pallas kernels, on_device(): pl.pallas_call(coulomb_kernel, out_shape=[whole, whole, whole, part, part...  8.9 us
    pallas_call x1, Pallas kernels, on_device(): pl.pallas_call(early_kernel, out_shape=[jax.ShapeDtypeStruct((NY - 1, row...  8.04 us
  transfers between devices with their start and end apart: 42, of which 21 were waited for; matrix products, arithmetic and copies ran while one was open for 1% of the time, Pallas kernels for 7%

profile of v3, /device:TPU:32, one launch (start us, length us, event | category | flops | bytes accessed | tf_op | source)
XLA Modules:
  0.0 185.3 jit_solution(7947557302315088053)
XLA Ops:
  2.7 4.3 %collective-permute-start.5 = (bf16[384,896]{1,0:T(8,128)(2,1)S(1)}, bf16[384,896]{1,0:T(8,128)(2,1)S(1)}, u32[]{:S(2)}, u32[]{:S(2)}) collective-permute-start(bf16[384,896]{1,0:T(8,128)(2,1)S(1)} %bitcast.29), channel_id=1, source_target_pairs={{0,33},{1,32},{32,1},{33,0},{2,35},{3,34},{34,3},{35,2},{4,37},{5,... | collective-permute-start | bytes 2064392 | tf_op jit(solution)/shard_map/gather/ppermute | solution.py:21
  10.2 10.6 %collective-permute-start.2 = (bf16[384,896]{1,0:T(8,128)(2,1)S(1)}, bf16[384,896]{1,0:T(8,128)(2,1)S(1)}, u32[]{:S(2)}, u32[]{:S(2)}) collective-permute-start(bf16[384,896]{1,0:T(8,128)(2,1)S(1)} %bitcast.30), channel_id=1, source_target_pairs={{0,1},{17,16},{2,3},{19,18},{4,5},{21,20},{6,7},{23,22},{8,9},{25,... | collective-permute-start | bytes 2064392 | tf_op jit(solution)/shard_map/gather/ppermute | solution.py:207
  22.5 4.2 %collective-permute-start.6 = (bf16[384,896]{1,0:T(8,128)(2,1)S(1)}, bf16[384,896]{1,0:T(8,128)(2,1)S(1)}, u32[]{:S(2)}, u32[]{:S(2)}) collective-permute-start(bf16[384,896]{1,0:T(8,128)(2,1)S(1)} %collective-permute-done.3.refs_1_), channel_id=1, source_target_pairs={{0,16},{16,0},{1,17},{17,1},{2,18},{18,2},{3,19},{19,3},{4,20},{20... | collective-permute-start | bytes 2064392 | tf_op jit(solution)/shard_map/gather/ppermute | solution.py:30
  34.7 8.0 %coulomb.2 = (f32[3,384,384]{2,1,0:T(8,128)}, bf16[1152,1792]{1,0:T(8,128)(2,1)}, bf16[1792,384]{1,0:T(8,128)(2,1)}, bf16[896,384]{1,0:T(8,128)(2,1)S(1)}) custom-call(bf16[384,896]{1,0:T(8,128)(2,1)S(1)} %bitcast.32, bf16[384,896]{1,0:T(8,128)(2,1)S(1)} %collective-permute-done.2.xlf, bf16[384,896]{1,0:T(8,128)(2,1)S(1)} %collective-permute-done.5.bof, ...), custom_call_target="tpu_custom_call" | custom-call | tf_op jit(solution)/shard_map/coulomb/pallas_call | solution.py:223
  43.3 5.8 %collective-permute-done.12.xh = bf16[384,896]{1,0:T(8,128)(2,1)S(1)} collective-permute-done((bf16[384,896]{1,0:T(8,128)(2,1)S(1)}, bf16[384,896]{1,0:T(8,128)(2,1)S(1)}, u32[]{:S(2)}, u32[]{:S(2)}) %collective-permute-start.12) | collective-permute-done | bytes 688160 | tf_op jit(solution)/shard_map/gather/ppermute | solution.py:21
  49.9 8.9 %coulomb.3 = (f32[384,384]{1,0:T(8,128)S(1)}, f32[384,384]{1,0:T(8,128)S(1)}, f32[384,384]{1,0:T(8,128)S(1)}, f32[192,384]{1,0:T(8,128)S(1)}, f32[192,384]{1,0:T...) custom-call(f32[3,384,384]{2,1,0:T(8,128)} %get-tuple-element.50.ear, ...), custom_call_target="tpu_custom_call" | custom-call | tf_op jit(solution)/shard_map/coulomb/pallas_call | solution.py:238
  64.1 3.8 %collective-permute-start.18 = (bf16[384,384]{1,0:T(8,128)(2,1)S(1)}, bf16[384,384]{1,0:T(8,128)(2,1)S(1)}, u32[]{:S(2)}, u32[]{:S(2)}) collective-permute-start(bf16[384,384]{1,0:T(8,128)(2,1)S(1)} %pad_maximum_fusion.1), channel_id=1, source_target_pairs={{0,14},{2,0},{4,2},{6,4},{8,6},{10,8},{12,10},{14,12},{1,15},{3,1}... | collective-permute-start | bytes 884744 | tf_op jit(solution)/shard_map/ring/ppermute | solution.py:26
  68.2 4.0 %collective-permute-done.18 = bf16[384,384]{1,0:T(8,128)(2,1)S(1)} collective-permute-done((bf16[384,384]{1,0:T(8,128)(2,1)S(1)}, bf16[384,384]{1,0:T(8,128)(2,1)S(1)}, u32[]{:S(2)}, u32[]{:S(2)}) %collective-permute-start.18) | collective-permute-done | bytes 294944 | tf_op jit(solution)/shard_map/ring/ppermute | solution.py:26
  72.2 3.8 %collective-permute-start.19 = (bf16[384,384]{1,0:T(8,128)(2,1)S(1)}, bf16[384,384]{1,0:T(8,128)(2,1)S(1)}, u32[]{:S(2)}, u32[]{:S(2)}) collective-permute-start(bf16[384,384]{1,0:T(8,128)(2,1)S(1)} %add_convert_fusion.5), channel_id=1, source_target_pairs={{0,14},{2,0},{4,2},{6,4},{8,6},{10,8},{12,10},{14,12},{1,15},{3,1}... | collective-permute-start | bytes 884744 | tf_op jit(solution)/shard_map/ring/ppermute | solution.py:26
  76.6 4.3 %collective-permute-done.19 = bf16[384,384]{1,0:T(8,128)(2,1)S(1)} collective-permute-done((bf16[384,384]{1,0:T(8,128)(2,1)S(1)}, bf16[384,384]{1,0:T(8,128)(2,1)S(1)}, u32[]{:S(2)}, u32[]{:S(2)}) %collective-permute-start.19) | collective-permute-done | bytes 294944 | tf_op jit(solution)/shard_map/ring/ppermute | solution.py:26
  81.0 4.2 %collective-permute-start.20 = (bf16[384,384]{1,0:T(8,128)(2,1)S(1)}, bf16[384,384]{1,0:T(8,128)(2,1)S(1)}, u32[]{:S(2)}, u32[]{:S(2)}) collective-permute-start(bf16[384,384]{1,0:T(8,128)(2,1)S(1)} %add_convert_fusion.4), channel_id=1, source_target_pairs={{0,14},{2,0},{4,2},{6,4},{8,6},{10,8},{12,10},{14,12},{1,15},{3,1}... | collective-permute-start | bytes 884744 | tf_op jit(solution)/shard_map/ring/ppermute | solution.py:26
  89.4 6.1 %collective-permute-done.16.up = bf16[384,384]{1,0:T(8,128)(2,1)S(1)} collective-permute-done((bf16[384,384]{1,0:T(8,128)(2,1)S(1)}, bf16[384,384]{1,0:T(8,128)(2,1)S(1)}, u32[]{:S(2)}, u32[]{:S(2)}) %collective-permute-start.16) | collective-permute-done | bytes 294944 | tf_op jit(solution)/shard_map/ring/ppermute | solution.py:26
  96.7 3.6 %collective-permute-start.22 = (bf16[2,192,384]{2,1,0:T(8,128)(2,1)S(1)}, bf16[2,192,384]{2,1,0:T(8,128)(2,1)S(1)}, u32[]{:S(2)}, u32[]{:S(2)}) collective-permute-start(bf16[2,192,384]{2,1,0:T(8,128)(2,1)S(1)} %combined.1.refs_0_), channel_id=1, source_target_pairs={{0,14},{2,0},{4,2},{6,4},{8,6},{10,8},{12,10},{14,12},{1,15},{3,1}... | collective-permute-start | bytes 884744 | tf_op jit(solution)/shard_map/combined/ppermute | solution.py:26
  100.3 7.4 %collective-permute-done.21.refs_1_ = bf16[2,192,384]{2,1,0:T(8,128)(2,1)S(1)} collective-permute-done((bf16[2,192,384]{2,1,0:T(8,128)(2,1)S(1)}, bf16[2,192,384]{2,1,0:T(8,128)(2,1)S(1)}, u32[]{:S(2)}, u32[]{:S(2)}) %collective-permute-start.21) | collective-permute-done | bytes 294944 | tf_op jit(solution)/shard_map/combined/ppermute | solution.py:26
  110.7 6.7 %collective-permute-done.23.refs_3_ = bf16[2,192,384]{2,1,0:T(8,128)(2,1)S(1)} collective-permute-done((bf16[2,192,384]{2,1,0:T(8,128)(2,1)S(1)}, bf16[2,192,384]{2,1,0:T(8,128)(2,1)S(1)}, u32[]{:S(2)}, u32[]{:S(2)}) %collective-permute-start.23) | collective-permute-done | bytes 294944 | tf_op jit(solution)/shard_map/combined/ppermute | solution.py:26
  120.3 4.7 %collective-permute-done.25.refs_5_ = bf16[2,192,384]{2,1,0:T(8,128)(2,1)S(1)} collective-permute-done((bf16[2,192,384]{2,1,0:T(8,128)(2,1)S(1)}, bf16[2,192,384]{2,1,0:T(8,128)(2,1)S(1)}, u32[]{:S(2)}, u32[]{:S(2)}) %collective-permute-start.25) | collective-permute-done | bytes 294944 | tf_op jit(solution)/shard_map/combined/ppermute | solution.py:26
  125.2 3.3 %collective-permute-start.28 = (bf16[2,96,384]{2,1,0:T(8,128)(2,1)S(1)}, bf16[2,96,384]{2,1,0:T(8,128)(2,1)S(1)}, u32[]{:S(2)}, u32[]{:S(2)}) collective-permute-start(bf16[2,96,384]{2,1,0:T(8,128)(2,1)S(1)} %slice.49), channel_id=1, source_target_pairs={{0,14},{2,0},{4,2},{6,4},{8,6},{10,8},{12,10},{14,12},{1,15},{3,1}... | collective-permute-start | bytes 442376 | tf_op jit(solution)/shard_map/combined/ppermute | solution.py:26
  131.5 5.9 %gamma.3 = (bf16[4,24,1792]{2,1,0:T(8,128)(2,1)S(1)}, bf16[4,24,1792]{2,1,0:T(8,128)(2,1)S(1)}, bf16[4,24,1792]{2,1,0:T(8,128)(2,1)S(1)}, f32[4,24,1792]{2,1,0:T(8,128)S(1)}) custom-call(bf16[2,192,384]{2,1,0:T(8,128)(2,1)S(1)} %combined.1.refs_0_, bf16[2,192,384]{2,1,0:T(8,128)(2,1)S(1)} %collective-permute-done.21.refs_1_, ...), custom_call_target="tpu_custom_call" | custom-call | tf_op jit(solution)/shard_map/gamma/pallas_call | solution.py:277
  137.4 3.6 %collective-permute-start.29 = (bf16[4,24,1792]{2,1,0:T(8,128)(2,1)S(1)}, bf16[4,24,1792]{2,1,0:T(8,128)(2,1)S(1)}, u32[]{:S(2)}, u32[]{:S(2)}) collective-permute-start(bf16[4,24,1792]{2,1,0:T(8,128)(2,1)S(1)} %get-tuple-element.74), channel_id=1, source_target_pairs={{0,33},{1,32},{32,1},{33,0},{2,35},{3,34},{34,3},{35,2},{4,37},{5,... | collective-permute-start | bytes 1032200 | tf_op jit(solution)/shard_map/gamma/ppermute | solution.py:21
  142.3 5.8 %gamma.2 = (f32[4,24,1792]{2,1,0:T(8,128)S(1)}, f32[4,24,1792]{2,1,0:T(8,128)S(1)}, f32[4,24,1792]{2,1,0:T(8,128)S(1)}, bf16[4,24,1792]{2,1,0:T(8,128)(2,1)S(1)}) custom-call(bf16[2,192,384]{2,1,0:T(8,128)(2,1)S(1)} %combined.1.refs_0_, bf16[2,192,384]{2,1,0:T(8,128)(2,1)S(1)} %collective-permute-done.21.refs_1_, ...), custom_call_target="tpu_custom_call" | custom-call | tf_op jit(solution)/shard_map/gamma/pallas_call | solution.py:277
  148.1 3.9 %collective-permute-done.30 = bf16[4,24,1792]{2,1,0:T(8,128)(2,1)S(1)} collective-permute-done((bf16[4,24,1792]{2,1,0:T(8,128)(2,1)S(1)}, bf16[4,24,1792]{2,1,0:T(8,128)(2,1)S(1)}, u32[]{:S(2)}, u32[]{:S(2)}) %collective-permute-start.30) | collective-permute-done | bytes 344096 | tf_op jit(solution)/shard_map/gamma/ppermute | solution.py:21
  154.4 6.2 %collective-permute-done.37 = bf16[4,24,1792]{2,1,0:T(8,128)(2,1)S(1)} collective-permute-done((bf16[4,24,1792]{2,1,0:T(8,128)(2,1)S(1)}, bf16[4,24,1792]{2,1,0:T(8,128)(2,1)S(1)}, u32[]{:S(2)}, u32[]{:S(2)}) %collective-permute-start.37) | collective-permute-done | bytes 344096 | tf_op jit(solution)/shard_map/gamma/ppermute | solution.py:21
  166.4 3.5 %collective-permute-start.40 = (bf16[24,1792]{1,0:T(8,128)(2,1)S(1)}, bf16[24,1792]{1,0:T(8,128)(2,1)S(1)}, u32[]{:S(2)}, u32[]{:S(2)}) collective-permute-start(bf16[24,1792]{1,0:T(8,128)(2,1)S(1)} %get-tuple-element.84), channel_id=1, source_target_pairs={{0,12},{2,14},{4,0},{6,2},{8,4},{10,6},{12,8},{14,10},{1,13},{3,15... | collective-permute-start | bytes 258056 | tf_op jit(solution)/shard_map/spread/ppermute | solution.py:26
  179.8 4.5 %collective-permute-done.35.refs_3_ = bf16[24,1792]{1,0:T(8,128)(2,1)S(1)} collective-permute-done((bf16[24,1792]{1,0:T(8,128)(2,1)S(1)}, bf16[24,1792]{1,0:T(8,128)(2,1)S(1)}, u32[]{:S(2)}, u32[]{:S(2)}) %collective-permute-start.35) | collective-permute-done | bytes 86048 | tf_op jit(solution)/shard_map/spread/ppermute | solution.py:26
  (100 shorter events, 57.9 us)
Async XLA Ops:
  2.7 19.8 %collective-permute-start.5 = (bf16[384,896]{1,0:T(8,128)(2,1)S(1)}, bf16[384,896]{1,0:T(8,128)(2,1)S(1)}, u32[]{:S(2)}, u32[]{:S(2)}) collective-permute-start(bf16[384,896]{1,0:T(8,128)(2,1)S(1)} %bitcast.29), channel_id=1, source_target_pairs={{0,33},{1,32},{32,1},{33,0},{2,35},{3,34},{34,3},{35,2},{4,37},{5,... | collective-permute-start | bytes 2064392 | tf_op jit(solution)/shard_map/gather/ppermute | solution.py:21
  7.0 15.5 %collective-permute-start.3 = (bf16[384,896]{1,0:T(8,128)(2,1)S(1)}, bf16[384,896]{1,0:T(8,128)(2,1)S(1)}, u32[]{:S(2)}, u32[]{:S(2)}) collective-permute-start(bf16[384,896]{1,0:T(8,128)(2,1)S(1)} %collective-permute-done.refs_0_), channel_id=1, source_target_pairs={{0,64},{64,128},{128,192},{192,0},{1,65},{65,129},{129,193},{193,1... | collective-permute-start | bytes 2064392 | tf_op jit(solution)/shard_map/gather/ppermute | solution.py:26
  8.6 13.9 %collective-permute-start.4 = (bf16[384,896]{1,0:T(8,128)(2,1)S(1)}, bf16[384,896]{1,0:T(8,128)(2,1)S(1)}, u32[]{:S(2)}, u32[]{:S(2)}) collective-permute-start(bf16[384,896]{1,0:T(8,128)(2,1)S(1)} %collective-permute-done.refs_0_), channel_id=1, source_target_pairs={{0,192},{64,0},{128,64},{192,128},{1,193},{65,1},{129,65},{193,129... | collective-permute-start | bytes 2064392 | tf_op jit(solution)/shard_map/gather/ppermute | solution.py:26
  10.2 19.1 %collective-permute-start.2 = (bf16[384,896]{1,0:T(8,128)(2,1)S(1)}, bf16[384,896]{1,0:T(8,128)(2,1)S(1)}, u32[]{:S(2)}, u32[]{:S(2)}) collective-permute-start(bf16[384,896]{1,0:T(8,128)(2,1)S(1)} %bitcast.30), channel_id=1, source_target_pairs={{0,1},{17,16},{2,3},{19,18},{4,5},{21,20},{6,7},{23,22},{8,9},{25,... | collective-permute-start | bytes 2064392 | tf_op jit(solution)/shard_map/gather/ppermute | solution.py:207
  20.9 10.2 %collective-permute-start.1 = (bf16[384,896]{1,0:T(8,128)(2,1)S(1)}, bf16[384,896]{1,0:T(8,128)(2,1)S(1)}, u32[]{:S(2)}, u32[]{:S(2)}) collective-permute-start(bf16[384,896]{1,0:T(8,128)(2,1)S(1)} %collective-permute-done.refs_0_), channel_id=1, source_target_pairs={{0,16},{16,0},{1,17},{17,1},{2,18},{18,2},{3,19},{19,3},{4,20},{20... | collective-permute-start | bytes 2064392 | tf_op jit(solution)/shard_map/gather/ppermute | solution.py:30
  22.5 11.4 %collective-permute-start.6 = (bf16[384,896]{1,0:T(8,128)(2,1)S(1)}, bf16[384,896]{1,0:T(8,128)(2,1)S(1)}, u32[]{:S(2)}, u32[]{:S(2)}) collective-permute-start(bf16[384,896]{1,0:T(8,128)(2,1)S(1)} %collective-permute-done.3.refs_1_), channel_id=1, source_target_pairs={{0,16},{16,0},{1,17},{17,1},{2,18},{18,2},{3,19},{19,3},{4,20},{20... | collective-permute-start | bytes 2064392 | tf_op jit(solution)/shard_map/gather/ppermute | solution.py:30
  26.8 15.9 %collective-permute-start.8 = (bf16[192,896]{1,0:T(8,128)(2,1)S(1)}, bf16[192,896]{1,0:T(8,128)(2,1)S(1)}, u32[]{:S(2)}, u32[]{:S(2)}) collective-permute-start(bf16[192,896]{1,0:T(8,128)(2,1)S(1)} %slice.36), channel_id=1, source_target_pairs={{0,64},{64,128},{128,192},{192,0},{1,65},{65,129},{129,193},{193,1... | collective-permute-start | bytes 1032200 | tf_op jit(solution)/shard_map/gather/ppermute | solution.py:26
  29.3 13.4 %collective-permute-start.9 = (bf16[192,896]{1,0:T(8,128)(2,1)S(1)}, bf16[192,896]{1,0:T(8,128)(2,1)S(1)}, u32[]{:S(2)}, u32[]{:S(2)}) collective-permute-start(bf16[192,896]{1,0:T(8,128)(2,1)S(1)} %slice.37), channel_id=1, source_target_pairs={{0,192},{64,0},{128,64},{192,128},{1,193},{65,1},{129,65},{193,129... | collective-permute-start | bytes 1032200 | tf_op jit(solution)/shard_map/gather/ppermute | solution.py:26
  31.1 18.0 %collective-permute-start.12 = (bf16[384,896]{1,0:T(8,128)(2,1)S(1)}, bf16[384,896]{1,0:T(8,128)(2,1)S(1)}, u32[]{:S(2)}, u32[]{:S(2)}) collective-permute-start(bf16[384,896]{1,0:T(8,128)(2,1)S(1)} %bitcast.31), channel_id=1, source_target_pairs={{0,32},{1,33},{32,0},{33,1},{2,34},{3,35},{34,2},{35,3},{4,36},{5,... | collective-permute-start | bytes 2064392 | tf_op jit(solution)/shard_map/gather/ppermute | solution.py:21
  59.0 9.0 %collective-permute-start.13 = (bf16[192,384]{1,0:T(8,128)(2,1)S(1)}, bf16[192,384]{1,0:T(8,128)(2,1)S(1)}, u32[]{:S(2)}, u32[]{:S(2)}) collective-permute-start(bf16[192,384]{1,0:T(8,128)(2,1)S(1)} %get-tuple-element.61), channel_id=1, source_target_pairs={{0,2},{2,4},{4,6},{6,8},{8,10},{10,12},{12,14},{14,0},{1,3},{3,5},... | collective-permute-start | bytes 442376 | tf_op jit(solution)/shard_map/ring/ppermute | solution.py:26
  76.5 9.4 %collective-permute-start.15 = (bf16[384,384]{1,0:T(8,128)(2,1)S(1)}, bf16[384,384]{1,0:T(8,128)(2,1)S(1)}, u32[]{:S(2)}, u32[]{:S(2)}) collective-permute-start(bf16[384,384]{1,0:T(8,128)(2,1)S(1)} %add_convert_fusion.7), channel_id=1, source_target_pairs={{0,2},{2,4},{4,6},{6,8},{8,10},{10,12},{12,14},{14,0},{1,3},{3,5},... | collective-permute-start | bytes 884744 | tf_op jit(solution)/shard_map/ring/ppermute | solution.py:26
  86.0 9.5 %collective-permute-start.16 = (bf16[384,384]{1,0:T(8,128)(2,1)S(1)}, bf16[384,384]{1,0:T(8,128)(2,1)S(1)}, u32[]{:S(2)}, u32[]{:S(2)}) collective-permute-start(bf16[384,384]{1,0:T(8,128)(2,1)S(1)} %add_convert_fusion.6), channel_id=1, source_target_pairs={{0,2},{2,4},{4,6},{6,8},{8,10},{10,12},{12,14},{14,0},{1,3},{3,5},... | collective-permute-start | bytes 884744 | tf_op jit(solution)/shard_map/ring/ppermute | solution.py:26
  96.6 11.1 %collective-permute-start.21 = (bf16[2,192,384]{2,1,0:T(8,128)(2,1)S(1)}, bf16[2,192,384]{2,1,0:T(8,128)(2,1)S(1)}, u32[]{:S(2)}, u32[]{:S(2)}) collective-permute-start(bf16[2,192,384]{2,1,0:T(8,128)(2,1)S(1)} %combined.1.refs_0_), channel_id=1, source_target_pairs={{0,2},{2,4},{4,6},{6,8},{8,10},{10,12},{12,14},{14,0},{1,3},{3,5},... | collective-permute-start | bytes 884744 | tf_op jit(solution)/shard_map/combined/ppermute | solution.py:26
  96.7 11.0 %collective-permute-start.22 = (bf16[2,192,384]{2,1,0:T(8,128)(2,1)S(1)}, bf16[2,192,384]{2,1,0:T(8,128)(2,1)S(1)}, u32[]{:S(2)}, u32[]{:S(2)}) collective-permute-start(bf16[2,192,384]{2,1,0:T(8,128)(2,1)S(1)} %combined.1.refs_0_), channel_id=1, source_target_pairs={{0,14},{2,0},{4,2},{6,4},{8,6},{10,8},{12,10},{14,12},{1,15},{3,1}... | collective-permute-start | bytes 884744 | tf_op jit(solution)/shard_map/combined/ppermute | solution.py:26
  107.7 9.7 %collective-permute-start.23 = (bf16[2,192,384]{2,1,0:T(8,128)(2,1)S(1)}, bf16[2,192,384]{2,1,0:T(8,128)(2,1)S(1)}, u32[]{:S(2)}, u32[]{:S(2)}) collective-permute-start(bf16[2,192,384]{2,1,0:T(8,128)(2,1)S(1)} %collective-permute-done.21.refs_1_), channel_id=1, source_target_pairs={{0,2},{2,4},{4,6},{6,8},{8,10},{10,12},{12,14},{14,0},{1,3},{3,5},... | collective-permute-start | bytes 884744 | tf_op jit(solution)/shard_map/combined/ppermute | solution.py:26
  107.7 9.7 %collective-permute-start.24 = (bf16[2,192,384]{2,1,0:T(8,128)(2,1)S(1)}, bf16[2,192,384]{2,1,0:T(8,128)(2,1)S(1)}, u32[]{:S(2)}, u32[]{:S(2)}) collective-permute-start(bf16[2,192,384]{2,1,0:T(8,128)(2,1)S(1)} %collective-permute-done.22.refs_2_), channel_id=1, source_target_pairs={{0,14},{2,0},{4,2},{6,4},{8,6},{10,8},{12,10},{14,12},{1,15},{3,1}... | collective-permute-start | bytes 884744 | tf_op jit(solution)/shard_map/combined/ppermute | solution.py:26
  137.4 10.7 %collective-permute-start.29 = (bf16[4,24,1792]{2,1,0:T(8,128)(2,1)S(1)}, bf16[4,24,1792]{2,1,0:T(8,128)(2,1)S(1)}, u32[]{:S(2)}, u32[]{:S(2)}) collective-permute-start(bf16[4,24,1792]{2,1,0:T(8,128)(2,1)S(1)} %get-tuple-element.74), channel_id=1, source_target_pairs={{0,33},{1,32},{32,1},{33,0},{2,35},{3,34},{34,3},{35,2},{4,37},{5,... | collective-permute-start | bytes 1032200 | tf_op jit(solution)/shard_map/gamma/ppermute | solution.py:21
  141.0 11.0 %collective-permute-start.30 = (bf16[4,24,1792]{2,1,0:T(8,128)(2,1)S(1)}, bf16[4,24,1792]{2,1,0:T(8,128)(2,1)S(1)}, u32[]{:S(2)}, u32[]{:S(2)}) collective-permute-start(bf16[4,24,1792]{2,1,0:T(8,128)(2,1)S(1)} %get-tuple-element.75), channel_id=1, source_target_pairs={{0,1},{1,0},{32,33},{33,32},{2,3},{3,2},{34,35},{35,34},{4,5},{5,4... | collective-permute-start | bytes 1032200 | tf_op jit(solution)/shard_map/gamma/ppermute | solution.py:21
  141.0 28.9 %collective-permute-start.32 = (bf16[4,24,1792]{2,1,0:T(8,128)(2,1)S(1)}, bf16[4,24,1792]{2,1,0:T(8,128)(2,1)S(1)}, u32[]{:S(2)}, u32[]{:S(2)}) collective-permute-start(bf16[4,24,1792]{2,1,0:T(8,128)(2,1)S(1)} %get-tuple-element.78), channel_id=1, source_target_pairs={{0,33},{1,32},{32,1},{33,0},{2,35},{3,34},{34,3},{35,2},{4,37},{5,... | collective-permute-start | bytes 1032200 | tf_op jit(solution)/shard_map/gamma/ppermute | solution.py:21
  152.9 20.0 %collective-permute-start.31 = (bf16[4,24,1792]{2,1,0:T(8,128)(2,1)S(1)}, bf16[4,24,1792]{2,1,0:T(8,128)(2,1)S(1)}, u32[]{:S(2)}, u32[]{:S(2)}) collective-permute-start(bf16[4,24,1792]{2,1,0:T(8,128)(2,1)S(1)} %add_convert_fusion.3), channel_id=1, source_target_pairs={{0,1},{1,0},{32,33},{33,32},{2,3},{3,2},{34,35},{35,34},{4,5},{5,4... | collective-permute-start | bytes 1032200 | tf_op jit(solution)/shard_map/gamma/ppermute | solution.py:21
  160.7 12.4 %collective-permute-start.38 = (bf16[24,1792]{1,0:T(8,128)(2,1)S(1)}, bf16[24,1792]{1,0:T(8,128)(2,1)S(1)}, u32[]{:S(2)}, u32[]{:S(2)}) collective-permute-start(bf16[24,1792]{1,0:T(8,128)(2,1)S(1)} %get-tuple-element.86), channel_id=1, source_target_pairs={{0,8},{2,10},{4,12},{6,14},{8,0},{10,2},{12,4},{14,6},{1,9},{3,11}... | collective-permute-start | bytes 258056 | tf_op jit(solution)/shard_map/spread/ppermute | solution.py:26
  163.2 10.4 %collective-permute-start.39 = (bf16[24,1792]{1,0:T(8,128)(2,1)S(1)}, bf16[24,1792]{1,0:T(8,128)(2,1)S(1)}, u32[]{:S(2)}, u32[]{:S(2)}) collective-permute-start(bf16[24,1792]{1,0:T(8,128)(2,1)S(1)} %get-tuple-element.85), channel_id=1, source_target_pairs={{0,10},{2,12},{4,14},{6,0},{8,2},{10,4},{12,6},{14,8},{1,11},{3,13... | collective-permute-start | bytes 258056 | tf_op jit(solution)/shard_map/spread/ppermute | solution.py:26
  166.4 9.9 %collective-permute-start.40 = (bf16[24,1792]{1,0:T(8,128)(2,1)S(1)}, bf16[24,1792]{1,0:T(8,128)(2,1)S(1)}, u32[]{:S(2)}, u32[]{:S(2)}) collective-permute-start(bf16[24,1792]{1,0:T(8,128)(2,1)S(1)} %get-tuple-element.84), channel_id=1, source_target_pairs={{0,12},{2,14},{4,0},{6,2},{8,4},{10,6},{12,8},{14,10},{1,13},{3,15... | collective-permute-start | bytes 258056 | tf_op jit(solution)/shard_map/spread/ppermute | solution.py:26
  173.6 10.8 %collective-permute-start.35 = (bf16[24,1792]{1,0:T(8,128)(2,1)S(1)}, bf16[24,1792]{1,0:T(8,128)(2,1)S(1)}, u32[]{:S(2)}, u32[]{:S(2)}) collective-permute-start(bf16[24,1792]{1,0:T(8,128)(2,1)S(1)} %get-tuple-element.87), channel_id=1, source_target_pairs={{0,6},{2,8},{4,10},{6,12},{8,14},{10,0},{12,2},{14,4},{1,7},{3,9},... | collective-permute-start | bytes 258056 | tf_op jit(solution)/shard_map/spread/ppermute | solution.py:26
  (23 other events, 207.3 us)

commit v4 on v2

--- a/solution.py
+++ b/solution.py
@@ -107,13 +107,10 @@
     def place(e, d):
         return lax.rem(e * NY + d + NZ - z, NZ)
 
-    def block(n, carry):
-        columns = many[pl.ds(pl.multiple_of(n * rows, 128), rows), :]
-        out[place(1, n)] = jnp.dot(columns, flipped[...], preferred_element_type=F32)
+    got = jnp.dot(many[...], flipped[...], preferred_element_type=F32)
+    for n in range(NY - 1):
+        out[place(1, n)] = got[n * rows:(n + 1) * rows]
         out[place(0, n)] = early[n]
-        return carry
-
-    lax.fori_loop(0, NY - 1, block, 0)
     out[place(0, NY - 1)] = jnp.dot(last[...], left[...], preferred_element_type=F32)
     out[place(1, NY - 1)] = jnp.dot(last[...], flipped[...], preferred_element_type=F32)
     low, high = slice(0, rows // 2), slice(rows // 2, rows)

time: 185 us -> 185 us (level)
  no operation moved by 1% of the time
where the time goes in v4:
time: 185 us; the launch traced here: 184 us
  starting transfers between devices  83 us (45%)
  waiting for transfers between devices  66.5 us (36%)
  Pallas kernels  30.7 us (17%)
  other arithmetic  2.53 us (1%)
    ppermute x27, starting transfers between devices, shift(): lax.ppermute(value, axis, [(i, (i + steps) % count) for i in range(count)])  51.5 us
    ppermute x27, waiting for transfers between devices, shift(): lax.ppermute(value, axis, [(i, (i + steps) % count) for i in range(count)])  50.7 us
    ppermute x8, starting transfers between devices, flip_x(): return lax.ppermute(value, X, [(i, i ^ bits) for i in range(NXH * NXL)])  15.3 us
    pallas_call x2, Pallas kernels, gamma_of(): pl.pallas_call(functools.partial(gamma_kernel, group=group), out_shape=[j...  12.3 us
    ppermute x8, waiting for transfers between devices, flip_x(): return lax.ppermute(value, X, [(i, i ^ bits) for i in range(NXH * NXL)])  11.6 us
    ppermute x1, starting transfers between devices, on_device(): xlf = lax.ppermute(own, ('core', 'xl'), [(0, 1), (3, 2)])  10.6 us
    pallas_call x1, Pallas kernels, on_device(): pl.pallas_call(coulomb_kernel, out_shape=[whole, whole, whole, part, part...  8.43 us
    pallas_call x1, Pallas kernels, on_device(): pl.pallas_call(early_kernel, out_shape=[jax.ShapeDtypeStruct((NY - 1, row...  8.04 us
  transfers between devices with their start and end apart: 42, of which 22 were waited for; matrix products, arithmetic and copies ran while one was open for 1% of the time, Pallas kernels for 8%

profile of v4, /device:TPU:32, one launch (start us, length us, event | category | flops | bytes accessed | tf_op | source)
XLA Modules:
  0.0 184.3 jit_solution(7854112234897394637)
XLA Ops:
  2.7 4.3 %collective-permute-start.5 = (bf16[384,896]{1,0:T(8,128)(2,1)S(1)}, bf16[384,896]{1,0:T(8,128)(2,1)S(1)}, u32[]{:S(2)}, u32[]{:S(2)}) collective-permute-start(bf16[384,896]{1,0:T(8,128)(2,1)S(1)} %bitcast.29), channel_id=1, source_target_pairs={{0,33},{1,32},{32,1},{33,0},{2,35},{3,34},{34,3},{35,2},{4,37},{5,... | collective-permute-start | bytes 2064392 | tf_op jit(solution)/shard_map/gather/ppermute | solution.py:21
  10.2 10.6 %collective-permute-start.2 = (bf16[384,896]{1,0:T(8,128)(2,1)S(1)}, bf16[384,896]{1,0:T(8,128)(2,1)S(1)}, u32[]{:S(2)}, u32[]{:S(2)}) collective-permute-start(bf16[384,896]{1,0:T(8,128)(2,1)S(1)} %bitcast.30), channel_id=1, source_target_pairs={{0,1},{17,16},{2,3},{19,18},{4,5},{21,20},{6,7},{23,22},{8,9},{25,... | collective-permute-start | bytes 2064392 | tf_op jit(solution)/shard_map/gather/ppermute | solution.py:204
  22.5 4.2 %collective-permute-start.6 = (bf16[384,896]{1,0:T(8,128)(2,1)S(1)}, bf16[384,896]{1,0:T(8,128)(2,1)S(1)}, u32[]{:S(2)}, u32[]{:S(2)}) collective-permute-start(bf16[384,896]{1,0:T(8,128)(2,1)S(1)} %collective-permute-done.3.refs_1_), channel_id=1, source_target_pairs={{0,16},{16,0},{1,17},{17,1},{2,18},{18,2},{3,19},{19,3},{4,20},{20... | collective-permute-start | bytes 2064392 | tf_op jit(solution)/shard_map/gather/ppermute | solution.py:30
  36.2 8.0 %coulomb.2 = (f32[3,384,384]{2,1,0:T(8,128)}, bf16[1152,1792]{1,0:T(8,128)(2,1)}, bf16[1792,384]{1,0:T(8,128)(2,1)}, bf16[896,384]{1,0:T(8,128)(2,1)S(1)}) custom-call(bf16[384,896]{1,0:T(8,128)(2,1)S(1)} %bitcast.32, bf16[384,896]{1,0:T(8,128)(2,1)S(1)} %collective-permute-done.2.xlf, bf16[384,896]{1,0:T(8,128)(2,1)S(1)} %collective-permute-done.5.bof, ...), custom_call_target="tpu_custom_call" | custom-call | tf_op jit(solution)/shard_map/coulomb/pallas_call | solution.py:220
  49.8 8.4 %coulomb.3 = (f32[384,384]{1,0:T(8,128)S(1)}, f32[384,384]{1,0:T(8,128)S(1)}, f32[384,384]{1,0:T(8,128)S(1)}, f32[192,384]{1,0:T(8,128)S(1)}, f32[192,384]{1,0:T...) custom-call(f32[3,384,384]{2,1,0:T(8,128)} %get-tuple-element.49.ear, ...), custom_call_target="tpu_custom_call" | custom-call | tf_op jit(solution)/shard_map/coulomb/pallas_call | solution.py:234
  60.5 3.9 %collective-permute-done.17 = bf16[192,384]{1,0:T(8,128)(2,1)S(1)} collective-permute-done((bf16[192,384]{1,0:T(8,128)(2,1)S(1)}, bf16[192,384]{1,0:T(8,128)(2,1)S(1)}, u32[]{:S(2)}, u32[]{:S(2)}) %collective-permute-start.17) | collective-permute-done | bytes 147488 | tf_op jit(solution)/shard_map/ring/ppermute | solution.py:26
  64.4 3.4 %collective-permute-start.18 = (bf16[384,384]{1,0:T(8,128)(2,1)S(1)}, bf16[384,384]{1,0:T(8,128)(2,1)S(1)}, u32[]{:S(2)}, u32[]{:S(2)}) collective-permute-start(bf16[384,384]{1,0:T(8,128)(2,1)S(1)} %pad_maximum_fusion.1), channel_id=1, source_target_pairs={{0,14},{2,0},{4,2},{6,4},{8,6},{10,8},{12,10},{14,12},{1,15},{3,1}... | collective-permute-start | bytes 884744 | tf_op jit(solution)/shard_map/ring/ppermute | solution.py:26
  68.3 5.3 %collective-permute-done.18 = bf16[384,384]{1,0:T(8,128)(2,1)S(1)} collective-permute-done((bf16[384,384]{1,0:T(8,128)(2,1)S(1)}, bf16[384,384]{1,0:T(8,128)(2,1)S(1)}, u32[]{:S(2)}, u32[]{:S(2)}) %collective-permute-start.18) | collective-permute-done | bytes 294944 | tf_op jit(solution)/shard_map/ring/ppermute | solution.py:26
  73.6 3.8 %collective-permute-start.19 = (bf16[384,384]{1,0:T(8,128)(2,1)S(1)}, bf16[384,384]{1,0:T(8,128)(2,1)S(1)}, u32[]{:S(2)}, u32[]{:S(2)}) collective-permute-start(bf16[384,384]{1,0:T(8,128)(2,1)S(1)} %add_convert_fusion.5), channel_id=1, source_target_pairs={{0,14},{2,0},{4,2},{6,4},{8,6},{10,8},{12,10},{14,12},{1,15},{3,1}... | collective-permute-start | bytes 884744 | tf_op jit(solution)/shard_map/ring/ppermute | solution.py:26
  78.0 4.5 %collective-permute-done.19 = bf16[384,384]{1,0:T(8,128)(2,1)S(1)} collective-permute-done((bf16[384,384]{1,0:T(8,128)(2,1)S(1)}, bf16[384,384]{1,0:T(8,128)(2,1)S(1)}, u32[]{:S(2)}, u32[]{:S(2)}) %collective-permute-start.19) | collective-permute-done | bytes 294944 | tf_op jit(solution)/shard_map/ring/ppermute | solution.py:26
  82.5 3.5 %collective-permute-start.20 = (bf16[384,384]{1,0:T(8,128)(2,1)S(1)}, bf16[384,384]{1,0:T(8,128)(2,1)S(1)}, u32[]{:S(2)}, u32[]{:S(2)}) collective-permute-start(bf16[384,384]{1,0:T(8,128)(2,1)S(1)} %add_convert_fusion.4), channel_id=1, source_target_pairs={{0,14},{2,0},{4,2},{6,4},{8,6},{10,8},{12,10},{14,12},{1,15},{3,1}... | collective-permute-start | bytes 884744 | tf_op jit(solution)/shard_map/ring/ppermute | solution.py:26
  86.7 3.6 %collective-permute-done.20.down = bf16[384,384]{1,0:T(8,128)(2,1)S(1)} collective-permute-done((bf16[384,384]{1,0:T(8,128)(2,1)S(1)}, bf16[384,384]{1,0:T(8,128)(2,1)S(1)}, u32[]{:S(2)}, u32[]{:S(2)}) %collective-permute-start.20) | collective-permute-done | bytes 294944 | tf_op jit(solution)/shard_map/ring/ppermute | solution.py:26
  90.4 4.2 %collective-permute-done.16.up = bf16[384,384]{1,0:T(8,128)(2,1)S(1)} collective-permute-done((bf16[384,384]{1,0:T(8,128)(2,1)S(1)}, bf16[384,384]{1,0:T(8,128)(2,1)S(1)}, u32[]{:S(2)}, u32[]{:S(2)}) %collective-permute-start.16) | collective-permute-done | bytes 294944 | tf_op jit(solution)/shard_map/ring/ppermute | solution.py:26
  99.0 5.6 %collective-permute-done.21.refs_1_ = bf16[2,192,384]{2,1,0:T(8,128)(2,1)S(1)} collective-permute-done((bf16[2,192,384]{2,1,0:T(8,128)(2,1)S(1)}, bf16[2,192,384]{2,1,0:T(8,128)(2,1)S(1)}, u32[]{:S(2)}, u32[]{:S(2)}) %collective-permute-start.21) | collective-permute-done | bytes 294944 | tf_op jit(solution)/shard_map/combined/ppermute | solution.py:26
  104.6 3.5 %collective-permute-start.24 = (bf16[2,192,384]{2,1,0:T(8,128)(2,1)S(1)}, bf16[2,192,384]{2,1,0:T(8,128)(2,1)S(1)}, u32[]{:S(2)}, u32[]{:S(2)}) collective-permute-start(bf16[2,192,384]{2,1,0:T(8,128)(2,1)S(1)} %collective-permute-done.22.refs_2_), channel_id=1, source_target_pairs={{0,14},{2,0},{4,2},{6,4},{8,6},{10,8},{12,10},{14,12},{1,15},{3,1}... | collective-permute-start | bytes 884744 | tf_op jit(solution)/shard_map/combined/ppermute | solution.py:26
  108.1 6.8 %collective-permute-done.23.refs_3_ = bf16[2,192,384]{2,1,0:T(8,128)(2,1)S(1)} collective-permute-done((bf16[2,192,384]{2,1,0:T(8,128)(2,1)S(1)}, bf16[2,192,384]{2,1,0:T(8,128)(2,1)S(1)}, u32[]{:S(2)}, u32[]{:S(2)}) %collective-permute-start.23) | collective-permute-done | bytes 294944 | tf_op jit(solution)/shard_map/combined/ppermute | solution.py:26
  114.9 3.7 %collective-permute-start.26 = (bf16[2,192,384]{2,1,0:T(8,128)(2,1)S(1)}, bf16[2,192,384]{2,1,0:T(8,128)(2,1)S(1)}, u32[]{:S(2)}, u32[]{:S(2)}) collective-permute-start(bf16[2,192,384]{2,1,0:T(8,128)(2,1)S(1)} %collective-permute-done.24.refs_4_), channel_id=1, source_target_pairs={{0,14},{2,0},{4,2},{6,4},{8,6},{10,8},{12,10},{14,12},{1,15},{3,1}... | collective-permute-start | bytes 884744 | tf_op jit(solution)/shard_map/combined/ppermute | solution.py:26
  118.6 6.1 %collective-permute-done.25.refs_5_ = bf16[2,192,384]{2,1,0:T(8,128)(2,1)S(1)} collective-permute-done((bf16[2,192,384]{2,1,0:T(8,128)(2,1)S(1)}, bf16[2,192,384]{2,1,0:T(8,128)(2,1)S(1)}, u32[]{:S(2)}, u32[]{:S(2)}) %collective-permute-start.25) | collective-permute-done | bytes 294944 | tf_op jit(solution)/shard_map/combined/ppermute | solution.py:26
  130.9 6.2 %gamma.3 = (bf16[4,24,1792]{2,1,0:T(8,128)(2,1)S(1)}, bf16[4,24,1792]{2,1,0:T(8,128)(2,1)S(1)}, bf16[4,24,1792]{2,1,0:T(8,128)(2,1)S(1)}, f32[4,24,1792]{2,1,0:T(8,128)S(1)}) custom-call(bf16[2,192,384]{2,1,0:T(8,128)(2,1)S(1)} %combined.1.refs_0_, bf16[2,192,384]{2,1,0:T(8,128)(2,1)S(1)} %collective-permute-done.21.refs_1_, ...), custom_call_target="tpu_custom_call" | custom-call | tf_op jit(solution)/shard_map/gamma/pallas_call | solution.py:273
  140.9 6.1 %gamma.2 = (f32[4,24,1792]{2,1,0:T(8,128)S(1)}, f32[4,24,1792]{2,1,0:T(8,128)S(1)}, f32[4,24,1792]{2,1,0:T(8,128)S(1)}, bf16[4,24,1792]{2,1,0:T(8,128)(2,1)S(1)}) custom-call(bf16[2,192,384]{2,1,0:T(8,128)(2,1)S(1)} %combined.1.refs_0_, bf16[2,192,384]{2,1,0:T(8,128)(2,1)S(1)} %collective-permute-done.21.refs_1_, ...), custom_call_target="tpu_custom_call" | custom-call | tf_op jit(solution)/shard_map/gamma/pallas_call | solution.py:273
  153.4 3.9 %collective-permute-done.37 = bf16[4,24,1792]{2,1,0:T(8,128)(2,1)S(1)} collective-permute-done((bf16[4,24,1792]{2,1,0:T(8,128)(2,1)S(1)}, bf16[4,24,1792]{2,1,0:T(8,128)(2,1)S(1)}, u32[]{:S(2)}, u32[]{:S(2)}) %collective-permute-start.37) | collective-permute-done | bytes 344096 | tf_op jit(solution)/shard_map/gamma/ppermute | solution.py:21
  161.6 3.4 %collective-permute-start.39 = (bf16[24,1792]{1,0:T(8,128)(2,1)S(1)}, bf16[24,1792]{1,0:T(8,128)(2,1)S(1)}, u32[]{:S(2)}, u32[]{:S(2)}) collective-permute-start(bf16[24,1792]{1,0:T(8,128)(2,1)S(1)} %get-tuple-element.81), channel_id=1, source_target_pairs={{0,10},{2,12},{4,14},{6,0},{8,2},{10,4},{12,6},{14,8},{1,11},{3,13... | collective-permute-start | bytes 258056 | tf_op jit(solution)/shard_map/spread/ppermute | solution.py:26
  168.2 3.4 %collective-permute-start.41 = (bf16[24,1792]{1,0:T(8,128)(2,1)S(1)}, bf16[24,1792]{1,0:T(8,128)(2,1)S(1)}, u32[]{:S(2)}, u32[]{:S(2)}) collective-permute-start(bf16[24,1792]{1,0:T(8,128)(2,1)S(1)} %get-tuple-element.79), channel_id=1, source_target_pairs={{0,14},{2,0},{4,2},{6,4},{8,6},{10,8},{12,10},{14,12},{1,15},{3,1}... | collective-permute-start | bytes 258056 | tf_op jit(solution)/shard_map/spread/ppermute | solution.py:26
  178.6 4.8 %collective-permute-done.35.refs_3_ = bf16[24,1792]{1,0:T(8,128)(2,1)S(1)} collective-permute-done((bf16[24,1792]{1,0:T(8,128)(2,1)S(1)}, bf16[24,1792]{1,0:T(8,128)(2,1)S(1)}, u32[]{:S(2)}, u32[]{:S(2)}) %collective-permute-start.35) | collective-permute-done | bytes 86048 | tf_op jit(solution)/shard_map/spread/ppermute | solution.py:26
  (100 shorter events, 62.7 us)
Async XLA Ops:
  2.7 19.8 %collective-permute-start.5 = (bf16[384,896]{1,0:T(8,128)(2,1)S(1)}, bf16[384,896]{1,0:T(8,128)(2,1)S(1)}, u32[]{:S(2)}, u32[]{:S(2)}) collective-permute-start(bf16[384,896]{1,0:T(8,128)(2,1)S(1)} %bitcast.29), channel_id=1, source_target_pairs={{0,33},{1,32},{32,1},{33,0},{2,35},{3,34},{34,3},{35,2},{4,37},{5,... | collective-permute-start | bytes 2064392 | tf_op jit(solution)/shard_map/gather/ppermute | solution.py:21
  7.0 15.5 %collective-permute-start.3 = (bf16[384,896]{1,0:T(8,128)(2,1)S(1)}, bf16[384,896]{1,0:T(8,128)(2,1)S(1)}, u32[]{:S(2)}, u32[]{:S(2)}) collective-permute-start(bf16[384,896]{1,0:T(8,128)(2,1)S(1)} %collective-permute-done.refs_0_), channel_id=1, source_target_pairs={{0,64},{64,128},{128,192},{192,0},{1,65},{65,129},{129,193},{193,1... | collective-permute-start | bytes 2064392 | tf_op jit(solution)/shard_map/gather/ppermute | solution.py:26
  8.6 13.9 %collective-permute-start.4 = (bf16[384,896]{1,0:T(8,128)(2,1)S(1)}, bf16[384,896]{1,0:T(8,128)(2,1)S(1)}, u32[]{:S(2)}, u32[]{:S(2)}) collective-permute-start(bf16[384,896]{1,0:T(8,128)(2,1)S(1)} %collective-permute-done.refs_0_), channel_id=1, source_target_pairs={{0,192},{64,0},{128,64},{192,128},{1,193},{65,1},{129,65},{193,129... | collective-permute-start | bytes 2064392 | tf_op jit(solution)/shard_map/gather/ppermute | solution.py:26
  10.2 19.1 %collective-permute-start.2 = (bf16[384,896]{1,0:T(8,128)(2,1)S(1)}, bf16[384,896]{1,0:T(8,128)(2,1)S(1)}, u32[]{:S(2)}, u32[]{:S(2)}) collective-permute-start(bf16[384,896]{1,0:T(8,128)(2,1)S(1)} %bitcast.30), channel_id=1, source_target_pairs={{0,1},{17,16},{2,3},{19,18},{4,5},{21,20},{6,7},{23,22},{8,9},{25,... | collective-permute-start | bytes 2064392 | tf_op jit(solution)/shard_map/gather/ppermute | solution.py:204
  22.5 12.9 %collective-permute-start.6 = (bf16[384,896]{1,0:T(8,128)(2,1)S(1)}, bf16[384,896]{1,0:T(8,128)(2,1)S(1)}, u32[]{:S(2)}, u32[]{:S(2)}) collective-permute-start(bf16[384,896]{1,0:T(8,128)(2,1)S(1)} %collective-permute-done.3.refs_1_), channel_id=1, source_target_pairs={{0,16},{16,0},{1,17},{17,1},{2,18},{18,2},{3,19},{19,3},{4,20},{20... | collective-permute-start | bytes 2064392 | tf_op jit(solution)/shard_map/gather/ppermute | solution.py:30
  29.3 18.4 %collective-permute-start.10 = (bf16[384,896]{1,0:T(8,128)(2,1)S(1)}, bf16[384,896]{1,0:T(8,128)(2,1)S(1)}, u32[]{:S(2)}, u32[]{:S(2)}) collective-permute-start(bf16[384,896]{1,0:T(8,128)(2,1)S(1)} %bitcast.31), channel_id=1, source_target_pairs={{0,32},{1,33},{32,0},{33,1},{2,34},{3,35},{34,2},{35,3},{4,36},{5,... | collective-permute-start | bytes 2064392 | tf_op jit(solution)/shard_map/gather/ppermute | solution.py:21
  32.1 12.2 %collective-permute-start.8 = (bf16[192,896]{1,0:T(8,128)(2,1)S(1)}, bf16[192,896]{1,0:T(8,128)(2,1)S(1)}, u32[]{:S(2)}, u32[]{:S(2)}) collective-permute-start(bf16[192,896]{1,0:T(8,128)(2,1)S(1)} %slice.36), channel_id=1, source_target_pairs={{0,64},{64,128},{128,192},{192,0},{1,65},{65,129},{129,193},{193,1... | collective-permute-start | bytes 1032200 | tf_op jit(solution)/shard_map/gather/ppermute | solution.py:26
  32.5 11.8 %collective-permute-start.9 = (bf16[192,896]{1,0:T(8,128)(2,1)S(1)}, bf16[192,896]{1,0:T(8,128)(2,1)S(1)}, u32[]{:S(2)}, u32[]{:S(2)}) collective-permute-start(bf16[192,896]{1,0:T(8,128)(2,1)S(1)} %slice.37), channel_id=1, source_target_pairs={{0,192},{64,0},{128,64},{192,128},{1,193},{65,1},{129,65},{193,129... | collective-permute-start | bytes 1032200 | tf_op jit(solution)/shard_map/gather/ppermute | solution.py:26
  58.4 9.7 %collective-permute-start.13 = (bf16[192,384]{1,0:T(8,128)(2,1)S(1)}, bf16[192,384]{1,0:T(8,128)(2,1)S(1)}, u32[]{:S(2)}, u32[]{:S(2)}) collective-permute-start(bf16[192,384]{1,0:T(8,128)(2,1)S(1)} %get-tuple-element.57), channel_id=1, source_target_pairs={{0,2},{2,4},{4,6},{6,8},{8,10},{10,12},{12,14},{14,0},{1,3},{3,5},... | collective-permute-start | bytes 442376 | tf_op jit(solution)/shard_map/ring/ppermute | solution.py:26
  64.4 9.1 %collective-permute-start.18 = (bf16[384,384]{1,0:T(8,128)(2,1)S(1)}, bf16[384,384]{1,0:T(8,128)(2,1)S(1)}, u32[]{:S(2)}, u32[]{:S(2)}) collective-permute-start(bf16[384,384]{1,0:T(8,128)(2,1)S(1)} %pad_maximum_fusion.1), channel_id=1, source_target_pairs={{0,14},{2,0},{4,2},{6,4},{8,6},{10,8},{12,10},{14,12},{1,15},{3,1}... | collective-permute-start | bytes 884744 | tf_op jit(solution)/shard_map/ring/ppermute | solution.py:26
  68.2 9.6 %collective-permute-start.14 = (bf16[384,384]{1,0:T(8,128)(2,1)S(1)}, bf16[384,384]{1,0:T(8,128)(2,1)S(1)}, u32[]{:S(2)}, u32[]{:S(2)}) collective-permute-start(bf16[384,384]{1,0:T(8,128)(2,1)S(1)} %pad_maximum_fusion), channel_id=1, source_target_pairs={{0,2},{2,4},{4,6},{6,8},{8,10},{10,12},{12,14},{14,0},{1,3},{3,5},... | collective-permute-start | bytes 884744 | tf_op jit(solution)/shard_map/ring/ppermute | solution.py:26
  95.6 9.0 %collective-permute-start.21 = (bf16[2,192,384]{2,1,0:T(8,128)(2,1)S(1)}, bf16[2,192,384]{2,1,0:T(8,128)(2,1)S(1)}, u32[]{:S(2)}, u32[]{:S(2)}) collective-permute-start(bf16[2,192,384]{2,1,0:T(8,128)(2,1)S(1)} %combined.1.refs_0_), channel_id=1, source_target_pairs={{0,2},{2,4},{4,6},{6,8},{8,10},{10,12},{12,14},{14,0},{1,3},{3,5},... | collective-permute-start | bytes 884744 | tf_op jit(solution)/shard_map/combined/ppermute | solution.py:26
  104.6 10.3 %collective-permute-start.23 = (bf16[2,192,384]{2,1,0:T(8,128)(2,1)S(1)}, bf16[2,192,384]{2,1,0:T(8,128)(2,1)S(1)}, u32[]{:S(2)}, u32[]{:S(2)}) collective-permute-start(bf16[2,192,384]{2,1,0:T(8,128)(2,1)S(1)} %collective-permute-done.21.refs_1_), channel_id=1, source_target_pairs={{0,2},{2,4},{4,6},{6,8},{8,10},{10,12},{12,14},{14,0},{1,3},{3,5},... | collective-permute-start | bytes 884744 | tf_op jit(solution)/shard_map/combined/ppermute | solution.py:26
  104.6 10.3 %collective-permute-start.24 = (bf16[2,192,384]{2,1,0:T(8,128)(2,1)S(1)}, bf16[2,192,384]{2,1,0:T(8,128)(2,1)S(1)}, u32[]{:S(2)}, u32[]{:S(2)}) collective-permute-start(bf16[2,192,384]{2,1,0:T(8,128)(2,1)S(1)} %collective-permute-done.22.refs_2_), channel_id=1, source_target_pairs={{0,14},{2,0},{4,2},{6,4},{8,6},{10,8},{12,10},{14,12},{1,15},{3,1}... | collective-permute-start | bytes 884744 | tf_op jit(solution)/shard_map/combined/ppermute | solution.py:26
  114.9 9.8 %collective-permute-start.25 = (bf16[2,192,384]{2,1,0:T(8,128)(2,1)S(1)}, bf16[2,192,384]{2,1,0:T(8,128)(2,1)S(1)}, u32[]{:S(2)}, u32[]{:S(2)}) collective-permute-start(bf16[2,192,384]{2,1,0:T(8,128)(2,1)S(1)} %collective-permute-done.23.refs_3_), channel_id=1, source_target_pairs={{0,2},{2,4},{4,6},{6,8},{8,10},{10,12},{12,14},{14,0},{1,3},{3,5},... | collective-permute-start | bytes 884744 | tf_op jit(solution)/shard_map/combined/ppermute | solution.py:26
  114.9 9.9 %collective-permute-start.26 = (bf16[2,192,384]{2,1,0:T(8,128)(2,1)S(1)}, bf16[2,192,384]{2,1,0:T(8,128)(2,1)S(1)}, u32[]{:S(2)}, u32[]{:S(2)}) collective-permute-start(bf16[2,192,384]{2,1,0:T(8,128)(2,1)S(1)} %collective-permute-done.24.refs_4_), channel_id=1, source_target_pairs={{0,14},{2,0},{4,2},{6,4},{8,6},{10,8},{12,10},{14,12},{1,15},{3,1}... | collective-permute-start | bytes 884744 | tf_op jit(solution)/shard_map/combined/ppermute | solution.py:26
  137.1 11.6 %collective-permute-start.29 = (bf16[4,24,1792]{2,1,0:T(8,128)(2,1)S(1)}, bf16[4,24,1792]{2,1,0:T(8,128)(2,1)S(1)}, u32[]{:S(2)}, u32[]{:S(2)}) collective-permute-start(bf16[4,24,1792]{2,1,0:T(8,128)(2,1)S(1)} %get-tuple-element.70), channel_id=1, source_target_pairs={{0,33},{1,32},{32,1},{33,0},{2,35},{3,34},{34,3},{35,2},{4,37},{5,... | collective-permute-start | bytes 1032200 | tf_op jit(solution)/shard_map/gamma/ppermute | solution.py:21
  138.6 10.1 %collective-permute-start.30 = (bf16[4,24,1792]{2,1,0:T(8,128)(2,1)S(1)}, bf16[4,24,1792]{2,1,0:T(8,128)(2,1)S(1)}, u32[]{:S(2)}, u32[]{:S(2)}) collective-permute-start(bf16[4,24,1792]{2,1,0:T(8,128)(2,1)S(1)} %get-tuple-element.71), channel_id=1, source_target_pairs={{0,1},{1,0},{32,33},{33,32},{2,3},{3,2},{34,35},{35,34},{4,5},{5,4... | collective-permute-start | bytes 1032200 | tf_op jit(solution)/shard_map/gamma/ppermute | solution.py:21
  140.2 28.1 %collective-permute-start.32 = (bf16[4,24,1792]{2,1,0:T(8,128)(2,1)S(1)}, bf16[4,24,1792]{2,1,0:T(8,128)(2,1)S(1)}, u32[]{:S(2)}, u32[]{:S(2)}) collective-permute-start(bf16[4,24,1792]{2,1,0:T(8,128)(2,1)S(1)} %get-tuple-element.74), channel_id=1, source_target_pairs={{0,33},{1,32},{32,1},{33,0},{2,35},{3,34},{34,3},{35,2},{4,37},{5,... | collective-permute-start | bytes 1032200 | tf_op jit(solution)/shard_map/gamma/ppermute | solution.py:21
  151.4 20.3 %collective-permute-start.31 = (bf16[4,24,1792]{2,1,0:T(8,128)(2,1)S(1)}, bf16[4,24,1792]{2,1,0:T(8,128)(2,1)S(1)}, u32[]{:S(2)}, u32[]{:S(2)}) collective-permute-start(bf16[4,24,1792]{2,1,0:T(8,128)(2,1)S(1)} %add_convert_fusion.3), channel_id=1, source_target_pairs={{0,1},{1,0},{32,33},{33,32},{2,3},{3,2},{34,35},{35,34},{4,5},{5,4... | collective-permute-start | bytes 1032200 | tf_op jit(solution)/shard_map/gamma/ppermute | solution.py:21
  158.6 13.3 %collective-permute-start.38 = (bf16[24,1792]{1,0:T(8,128)(2,1)S(1)}, bf16[24,1792]{1,0:T(8,128)(2,1)S(1)}, u32[]{:S(2)}, u32[]{:S(2)}) collective-permute-start(bf16[24,1792]{1,0:T(8,128)(2,1)S(1)} %get-tuple-element.82), channel_id=1, source_target_pairs={{0,8},{2,10},{4,12},{6,14},{8,0},{10,2},{12,4},{14,6},{1,9},{3,11}... | collective-permute-start | bytes 258056 | tf_op jit(solution)/shard_map/spread/ppermute | solution.py:26
  161.6 12.5 %collective-permute-start.39 = (bf16[24,1792]{1,0:T(8,128)(2,1)S(1)}, bf16[24,1792]{1,0:T(8,128)(2,1)S(1)}, u32[]{:S(2)}, u32[]{:S(2)}) collective-permute-start(bf16[24,1792]{1,0:T(8,128)(2,1)S(1)} %get-tuple-element.81), channel_id=1, source_target_pairs={{0,10},{2,12},{4,14},{6,0},{8,2},{10,4},{12,6},{14,8},{1,11},{3,13... | collective-permute-start | bytes 258056 | tf_op jit(solution)/shard_map/spread/ppermute | solution.py:26
  165.0 11.9 %collective-permute-start.40 = (bf16[24,1792]{1,0:T(8,128)(2,1)S(1)}, bf16[24,1792]{1,0:T(8,128)(2,1)S(1)}, u32[]{:S(2)}, u32[]{:S(2)}) collective-permute-start(bf16[24,1792]{1,0:T(8,128)(2,1)S(1)} %get-tuple-element.80), channel_id=1, source_target_pairs={{0,12},{2,14},{4,0},{6,2},{8,4},{10,6},{12,8},{14,10},{1,13},{3,15... | collective-permute-start | bytes 258056 | tf_op jit(solution)/shard_map/spread/ppermute | solution.py:26
  174.1 9.3 %collective-permute-start.35 = (bf16[24,1792]{1,0:T(8,128)(2,1)S(1)}, bf16[24,1792]{1,0:T(8,128)(2,1)S(1)}, u32[]{:S(2)}, u32[]{:S(2)}) collective-permute-start(bf16[24,1792]{1,0:T(8,128)(2,1)S(1)} %get-tuple-element.83), channel_id=1, source_target_pairs={{0,6},{2,8},{4,10},{6,12},{8,14},{10,0},{12,2},{14,4},{1,7},{3,9},... | collective-permute-start | bytes 258056 | tf_op jit(solution)/shard_map/spread/ppermute | solution.py:26
  (23 other events, 199.6 us)
